TPU v7x, 768 devices: a whole 4x8x12 slice. The times are simulated.
768 devices in a mesh: dp: 192 (over y, z, core), expert: 4 (over x).
Axes of the slice: x: 4, y: 8, z: 12, core: 2. Of those that a mesh axis runs over, the one named last changes fastest.
Arguments:
- tokens: bfloat16 [128, 6144], P('expert', 'dp'), may hold values from -6 to 6
- routes: int32 [128, 2], P('expert'), may hold values from 0 to 3, all different within a row; in each aligned block of 32 rows (0 to 31, 32 to 63, ...) at most 24 rows name the same one
- probs: float32 [128, 2], P('expert'), may hold values from 0.1 to 0.9
- w_gate: bfloat16 [4, 12288, 6144], P('expert', 'dp'), may hold values from -0.078125 to 0.078125
- w_up: bfloat16 [4, 12288, 6144], P('expert', 'dp'), may hold values from -0.078125 to 0.078125
- w_down: bfloat16 [4, 12288, 6144], P('expert', 'dp'), may hold values from -0.0546875 to 0.0546875
- grad_out: bfloat16 [128, 6144], P('expert', 'dp'), may hold values from -6 to 6
Outputs:
- mixed: bfloat16 [128, 6144], P('expert', 'dp')
- grad_tokens: bfloat16 [128, 6144], P('expert', 'dp')
- grad_gate: bfloat16 [4, 12288, 6144], P('expert', 'dp')
- grad_up: bfloat16 [4, 12288, 6144], P('expert', 'dp')
- grad_down: bfloat16 [4, 12288, 6144], P('expert', 'dp')
Inputs may be any that keep to these rules, and one draw needn't show every extreme that they name: `routes`: each row names 2 different experts; within the rows of one index of expert (aligned blocks of 32 rows) no expert is named by more than 24 rows, and in some block one expert is named by exactly 24.
All inputs are finite; a program needn't handle non-finite values.
Results may differ from a plain program's by a relative error of at most 0.01.
Values may be sent and summed in bfloat16 or wider, within the bound.
No kernel may reach another device: no remote copies, remote signals or barrier semaphores. Data moves between devices by JAX's collectives and lax.ppermute only.
A program may use at most 32 MiB of HBM per device.

v0:
```python
import jax
import jax.numpy as jnp
from jax import lax
from jax.sharding import PartitionSpec as P


def tdot(a, b):
    return lax.dot_general(a, b, (((0,), (0,)), ((), ())), preferred_element_type=jnp.float32)


def ndot(a, b):
    return lax.dot_general(a, b, (((1,), (1,)), ((), ())), preferred_element_type=jnp.float32)


def on_device(tokens, routes, probs, w_gate, w_up, w_down, grad_out):
    experts = lax.axis_size("expert")
    tok_count = tokens.shape[0]
    narrow = tokens.shape[1]
    labels = lax.broadcasted_iota(jnp.int32, (experts, tok_count, routes.shape[1]), 0)
    hits = routes[None] == labels
    mask = jnp.sum(hits.astype(jnp.float32), axis=2)
    share = jnp.sum(jnp.where(hits, probs[None], 0.0), axis=2)
    cot_all = (share[:, :, None] * grad_out[None].astype(jnp.float32)).astype(jnp.bfloat16)
    sent_rows = jnp.where(mask[:, :, None] > 0.5, tokens[None], jnp.zeros_like(tokens)[None])
    got_rows, got_cot = (
        lax.all_to_all(sent_rows, "expert", split_axis=0, concat_axis=0, tiled=True),
        lax.all_to_all(cot_all, "expert", split_axis=0, concat_axis=0, tiled=True),
    )
    row_count = experts * tok_count
    got_rows = got_rows.reshape(row_count, narrow)
    got_cot = got_cot.reshape(row_count, narrow)
    gate_w = w_gate[0]
    up_w = w_up[0]
    down_w = w_down[0]
    hidden_count = gate_w.shape[0]
    piece = lax.all_gather(got_rows, "dp", axis=1, tiled=True)
    gate = ndot(piece, gate_w)
    upper = ndot(piece, up_w)
    full_cot = lax.all_gather(got_cot, "dp", axis=1, tiled=True)
    sig = jax.nn.sigmoid(gate)
    act = gate * sig
    hidden = (act * upper).astype(jnp.bfloat16)
    part_out = jnp.dot(hidden, down_w, preferred_element_type=jnp.float32)
    grad_down = tdot(hidden, full_cot).astype(jnp.bfloat16)
    dhid = ndot(full_cot, down_w)
    dgate = (dhid * upper * sig * (1.0 + gate * (1.0 - sig))).astype(jnp.bfloat16)
    dup = (dhid * act).astype(jnp.bfloat16)
    joined = jnp.concatenate([dgate, dup], axis=1)
    paired = tdot(joined, lax.all_gather(got_rows, "dp", axis=1, tiled=True))
    grad_gate = paired[:hidden_count].astype(jnp.bfloat16)
    grad_up = paired[hidden_count:].astype(jnp.bfloat16)
    part_back = jnp.dot(dgate, gate_w, preferred_element_type=jnp.float32) + jnp.dot(
        dup, up_w, preferred_element_type=jnp.float32
    )
    out_sum, back_sum = (
        lax.psum_scatter(part_out, "dp", scatter_dimension=1, tiled=True),
        lax.psum_scatter(part_back, "dp", scatter_dimension=1, tiled=True),
    )
    expert_out = out_sum.astype(jnp.bfloat16).reshape(experts, tok_count, narrow)
    expert_back = back_sum.astype(jnp.bfloat16).reshape(experts, tok_count, narrow)
    ret_out, ret_back = (
        lax.all_to_all(expert_out, "expert", split_axis=0, concat_axis=0, tiled=True),
        lax.all_to_all(expert_back, "expert", split_axis=0, concat_axis=0, tiled=True),
    )
    placed_out = ret_out.astype(jnp.float32)
    placed_back = ret_back.astype(jnp.float32)
    mixed = jnp.sum(share[:, :, None] * placed_out, axis=0).astype(jnp.bfloat16)
    grad_tokens = jnp.sum(placed_back, axis=0).astype(jnp.bfloat16)
    return (mixed, grad_tokens, grad_gate[None], grad_up[None], grad_down[None])


def solution(mesh):
    placed = (
        P("expert", "dp"),
        P("expert", None),
        P("expert", None),
        P("expert", "dp", None),
        P("expert", "dp", None),
        P("expert", "dp", None),
        P("expert", "dp"),
    )
    return jax.shard_map(
        on_device,
        mesh=mesh,
        in_specs=placed,
        out_specs=(
            P("expert", "dp"),
            P("expert", "dp"),
            P("expert", "dp", None),
            P("expert", "dp", None),
            P("expert", "dp", None),
        ),
        check_vma=False,
    )
```

profile of v0, /device:TPU:1, one launch (start us, length us, event | category | flops | bytes accessed | tf_op | source)
XLA Modules:
  0.0 886.4 jit_solution(8890848551445593229)
XLA Ops:
  7.2 0.0 copy-start
  7.2 0.0 copy-start.3
  7.2 0.0 all-gather.3.cloned.1.call-start
  7.2 0.8 select_reduce_fusion
  8.1 0.8 copy.59
  8.8 0.1 reshape.36
  9.0 8.8 all_to_all.20
  17.8 0.1 reshape.37
  17.9 0.7 reshape.32
  18.6 0.0 all-gather.3.cloned.1.call-update
  18.6 0.0 all-gather.5.cloned.1.call-start
  18.7 0.8 copy.63
  19.4 0.1 reshape.40
  19.5 6.5 all_to_all.21
  26.1 0.1 reshape.41
  26.2 0.7 reshape.34
  26.9 0.0 all-gather.5.cloned.1.call-update
  26.9 0.0 reduce-scatter.5.cloned.1.call-start
  26.9 109.5 %all-gather.3.cloned.1.call-done = bf16[128,6144]{0,1:T(8,128)(2,1)} async-done(((bf16[128,32]{0,1:T(8,128)(2,1)}), bf16[128,6144]{0,1:T(8,128)(2,1)}) %all-gather.3.cloned.1.call-update) | async-done | bytes 1572880 | tf_op jit(solution)/shard_map/all_gather | solution.py:36
  136.5 0.0 copy-start.1
  136.5 2.2 fusion.10
  138.7 0.0 copy-done.3
  138.7 0.0 copy-done.1
  138.7 0.4 fusion.6
  139.1 110.4 %all-gather.5.cloned.1.call-done = bf16[128,6144]{0,1:T(8,128)(2,1)} async-done(((bf16[128,32]{0,1:T(8,128)(2,1)}), bf16[128,6144]{0,1:T(8,128)(2,1)}) %all-gather.5.cloned.1.call-update) | async-done | bytes 1572880 | tf_op jit(solution)/shard_map/all_gather | solution.py:39
  249.5 0.0 copy-done
  249.5 0.0 copy-start.4
  249.5 1.9 multiply_convert_fusion.1
  251.4 0.0 copy-done.4
  251.4 0.7 fusion.8
  252.2 2.4 convolution_add_fusion
  254.6 0.0 reduce-scatter.5.cloned.1.call-update
  254.6 0.0 reduce-scatter.3.cloned.1.call-start
  254.7 2.4 fusion.3
  257.1 0.0 reduce-scatter.3.cloned.1.call-update
  257.1 0.6 convolution_convert_fusion
  257.7 0.0 copy-start.2
  257.7 1.2 slice_bitcast_fusion
  258.9 299.7 %reduce-scatter.5.cloned.1.call-done = f32[128,32]{0,1:T(8,128)} async-done(((f32[128,6144]{0,1:T(8,128)}), f32[128,32]{0,1:T(8,128)}) %reduce-scatter.5.cloned.1.call-update) | async-done | bytes 16400 | tf_op jit(solution)/shard_map/reduce_scatter | solution.py:57
  558.6 0.7 convert_element_type.47
  559.3 0.1 reshape.35
  559.4 0.7 reshape.42
  560.1 4.0 all-to-all-start.3
  564.1 0.0 copy-done.2
  564.1 1.5 fusion
  565.6 303.8 %reduce-scatter.3.cloned.1.call-done = f32[128,32]{0,1:T(8,128)} async-done(((f32[128,6144]{0,1:T(8,128)}), f32[128,32]{0,1:T(8,128)}) %reduce-scatter.3.cloned.1.call-update) | async-done | bytes 16400 | tf_op jit(solution)/shard_map/reduce_scatter | solution.py:56
  869.4 0.7 convert_element_type.40
  870.2 0.1 reshape.33
  870.3 0.7 reshape.38
  871.0 0.0 all-to-all-done.3
  871.0 4.0 all-to-all-start.1
  874.9 0.1 reshape.43
  875.1 0.7 copy.68
  875.7 3.4 all-to-all-done.1
  879.1 0.1 reshape.39
  879.2 0.7 copy.67
  (9 shorter events, 0.1 us)
Async XLA Ops:
  7.2 242.4 %copy-start = (bf16[1,64,6144]{2,1,0:T(8,128)(2,1)S(1)}, bf16[1,64,6144]{2,1,0:T(8,128)(2,1)}, u32[]{:S(2)}) copy-start(bf16[1,64,6144]{2,1,0:T(8,128)(2,1)} %param.12) | copy-start | bytes 2359300
  7.2 131.5 %copy-start.3 = (bf16[1,64,6144]{2,1,0:T(8,128)(2,1)S(1)}, bf16[1,64,6144]{2,1,0:T(8,128)(2,1)}, u32[]{:S(2)}) copy-start(bf16[1,64,6144]{2,1,0:T(8,128)(2,1)} %param.11) | copy-start | bytes 2359300
  7.2 129.3 %all-gather.3.cloned.1.call-start = ((), (), s32[]{:S(2)}) async-start(), calls=%async_computation.6 | async-start | bytes 1581056 | tf_op jit(solution)/shard_map/all_gather | solution.py:36
  18.6 230.9 %all-gather.5.cloned.1.call-start = ((), (), s32[]{:S(2)}) async-start(), calls=%async_computation.8 | async-start | bytes 1581056 | tf_op jit(solution)/shard_map/all_gather | solution.py:39
  26.9 531.7 %reduce-scatter.5.cloned.1.call-start = ((), (), s32[]{:S(2)}) async-start(), calls=%async_computation.9 | async-start | bytes 3162112 | tf_op jit(solution)/shard_map/reduce_scatter | solution.py:57
  136.5 2.2 copy-start.1
  249.5 1.9 copy-start.4
  254.6 614.8 %reduce-scatter.3.cloned.1.call-start = ((), (), s32[]{:S(2)}) async-start(), calls=%async_computation.7 | async-start | bytes 3162112 | tf_op jit(solution)/shard_map/reduce_scatter | solution.py:56
  257.7 306.4 %copy-start.2 = (bf16[128,6144]{0,1:T(8,128)(2,1)S(1)}, bf16[128,6144]{0,1:T(8,128)(2,1)}, u32[]{:S(2)}) copy-start(bf16[128,6144]{0,1:T(8,128)(2,1)} %all-gather.5.cloned.1.call-done) | copy-start | bytes 4718596
  560.1 310.9 %all-to-all-start.3 = ((bf16[4,2,512]{2,1,0:T(2,128)(2,1)}), bf16[4,2,512]{2,1,0:T(2,128)(2,1)S(1)}, u32[]{:S(2)}, u32[]{:S(2)}) async-start(bf16[4,2,512]{2,1,0:T(2,128)(2,1)} %reshape.42), calls=%async_computation.5 | async-start | bytes 16384 | tf_op jit(solution)/shard_map/all_to_all | solution.py:63
  871.0 8.1 all-to-all-start.1
Sparse Core Ops, SparseCore 0:
  18.7 117.7 all-gather.2
  140.8 108.7 all-gather.4
  255.0 303.5 reduce-scatter.4
  564.8 304.6 reduce-scatter.2
where the time goes:
time: 888 us; the launch traced here: 886 us
  waiting for transfers between devices  827 us (93%)
  blocking collectives  15.3 us (2%)
  between operations  13.9 us (2%)
  matrix products  12.1 us (1%)
    reduce_scatter x1, waiting for transfers between devices, on_device(): lax.psum_scatter(part_out, 'dp', scatter_dimension=1, tiled=True)  304 us
    reduce_scatter x1, waiting for transfers between devices, on_device(): lax.psum_scatter(part_back, 'dp', scatter_dimension=1, tiled=True)  300 us
    all_gather x1, waiting for transfers between devices, on_device(): full_cot = lax.all_gather(got_cot, 'dp', axis=1, tiled=True)  110 us
    all_gather x1, waiting for transfers between devices, on_device(): piece = lax.all_gather(got_rows, 'dp', axis=1, tiled=True)  110 us
  transfers between devices with their start and end apart: 6, of which 5 were waited for; matrix products, arithmetic and copies ran while one was open for 2% of the time, Pallas kernels for 0%

commit v1 on v0

v1 whole, which is shorter than its diff:
```python
import jax
import jax.numpy as jnp
from jax import lax
from jax.sharding import Mesh, PartitionSpec as P

CORES = 2
COLUMNS = 8
SLOTS = 24


def tdot(a, b):
    return lax.dot_general(a, b, (((0,), (0,)), ((), ())), preferred_element_type=jnp.float32)


def ndot(a, b):
    return lax.dot_general(a, b, (((1,), (1,)), ((), ())), preferred_element_type=jnp.float32)


def swap(a, axis):
    return lax.all_to_all(a, axis, split_axis=0, concat_axis=0, tiled=True)


def on_device(tokens, routes, probs, w_gate, w_up, w_down, grad_out):
    bf16, f32 = jnp.bfloat16, jnp.float32
    experts = lax.axis_size("expert")
    depth = lax.axis_size("z")
    columns = lax.axis_size("y")
    cores = lax.axis_size("core")
    first = lax.axis_index("core") == 0
    count, narrow = tokens.shape
    wide = depth * cores * narrow
    width = columns * wide
    rows_of = experts * SLOTS

    labels = lax.broadcasted_iota(jnp.int32, (experts, count, routes.shape[1]), 0)
    hits = routes[None] == labels
    mask = jnp.any(hits, axis=2)
    share = jnp.sum(jnp.where(hits, probs[None], 0.0), axis=2)
    earlier = lax.broadcasted_iota(jnp.int32, (count, count), 1) < lax.broadcasted_iota(jnp.int32, (count, count), 0)
    place = jnp.sum(jnp.where(earlier[None] & mask[:, None, :], 1, 0), axis=2)
    slots = lax.broadcasted_iota(jnp.int32, (experts, SLOTS, count), 1)
    chosen = (place[:, None, :] == slots) & mask[:, None, :]
    pick = chosen.reshape(rows_of, count).astype(bf16)
    weight = jnp.where(first, jnp.ones_like(share), share)
    slot_weight = jnp.sum(jnp.where(chosen, weight[:, None, :], 0.0), axis=2).reshape(rows_of, 1)

    both = jnp.stack([tokens, grad_out]).reshape(1, cores, count * narrow // 128, 128)
    sent = jnp.broadcast_to(both, (depth,) + both.shape[1:]).reshape(depth * cores, -1, 128)
    got = swap(sent, ("z", "core")).reshape(depth * cores, count, narrow)
    mine = got.transpose(1, 0, 2).reshape(count, wide)

    packed = (jnp.dot(pick, mine, preferred_element_type=f32) * slot_weight).astype(bf16)
    sent = jnp.broadcast_to(packed.reshape(1, experts, SLOTS, wide), (columns, experts, SLOTS, wide))
    got = swap(sent.reshape(columns * experts, SLOTS, wide), ("y", "expert"))
    mine = got.reshape(columns, rows_of, wide).transpose(1, 0, 2).reshape(rows_of, width)
    other = lax.ppermute(mine, "core", [(0, 1), (1, 0)])
    rows = jnp.where(first, mine, other)
    cot = jnp.where(first, other, mine)

    gate_w, up_w, down_w = w_gate[0], w_up[0], w_down[0]
    hidden_count = gate_w.shape[0]
    gate = ndot(rows, gate_w)
    upper = ndot(rows, up_w)
    dhid = ndot(cot, down_w)
    sig = jax.nn.sigmoid(gate)
    act = gate * sig
    hidden = (act * upper).astype(bf16)
    dgate = (dhid * upper * sig * (1.0 + gate * (1.0 - sig))).astype(bf16)
    dup = (dhid * act).astype(bf16)
    part_out = jnp.dot(hidden, down_w, preferred_element_type=f32)
    part_back = jnp.dot(dgate, gate_w, preferred_element_type=f32) + jnp.dot(dup, up_w, preferred_element_type=f32)

    away = jnp.where(first, part_back, part_out).astype(bf16)
    kept = jnp.where(first, part_out, part_back)
    total = (kept + lax.ppermute(away, "core", [(0, 1), (1, 0)]).astype(f32)).astype(bf16)
    sent = total.reshape(rows_of, columns, wide).transpose(1, 0, 2).reshape(columns * experts, SLOTS, wide)
    got = swap(sent, ("y", "expert")).reshape(columns, experts, SLOTS, wide)
    summed = jnp.sum(got.astype(f32), axis=0)
    back_weight = jnp.where(first, share, mask.astype(f32))
    spread = jnp.where(chosen, back_weight[:, None, :], 0.0).reshape(rows_of, count)
    placed = lax.dot_general(
        spread, summed.reshape(rows_of, wide), (((0,), (0,)), ((), ())),
        precision=lax.Precision.HIGHEST, preferred_element_type=f32,
    ).astype(bf16)
    sent = placed.reshape(count, depth * cores, narrow).transpose(1, 0, 2).reshape(depth * cores, -1, 128)
    got = swap(sent, ("z", "core")).reshape(depth, cores, count, narrow)
    result = jnp.sum(got.astype(f32), axis=0).astype(bf16)

    grad_down = tdot(hidden, cot).astype(bf16)
    paired = tdot(jnp.concatenate([dgate, dup], axis=1), rows)
    grad_gate = paired[:hidden_count].astype(bf16)
    grad_up = paired[hidden_count:].astype(bf16)
    return (result[0], result[1], grad_gate[None], grad_up[None], grad_down[None])


def solution(mesh):
    shape = mesh.devices.shape
    split = mesh.devices.reshape(COLUMNS, shape[0] // (COLUMNS * CORES), CORES, shape[1])
    fine = Mesh(split, ("y", "z", "core", "expert"))
    dp = ("y", "z", "core")
    placed = (
        P("expert", dp),
        P("expert", None),
        P("expert", None),
        P("expert", dp, None),
        P("expert", dp, None),
        P("expert", dp, None),
        P("expert", dp),
    )
    return jax.shard_map(
        on_device,
        mesh=fine,
        in_specs=placed,
        out_specs=(P("expert", dp), P("expert", dp), P("expert", dp, None), P("expert", dp, None), P("expert", dp, None)),
        check_vma=False,
    )
```

time: 888 us -> 143 us (0.16)
  waiting for transfers between devices: 827 us -> 50.3 us
  blocking collectives: 15.3 us -> 41.2 us
  starting transfers between devices: 8.1 us -> 33.4 us
  between operations: 13.9 us -> 0.88 us
    reduce_scatter x2 -> x0, waiting for transfers between devices: 604 us -> none  [the longest x1 304 us: on_device(): lax.psum_scatter(part_out, 'dp', scatter_dimension=1, tiled=True)]
    all_gather x2 -> x0, waiting for transfers between devices: 220 us -> none  [the longest x1 110 us: on_device(): full_cot = lax.all_gather(got_cot, 'dp', axis=1, tiled=True)]
    all_to_all x2 -> x3, waiting for transfers between devices: 3.38 us -> 45.4 us  [swap(): return lax.all_to_all(a, axis, split_axis=0, concat_axis=0, tiled=True)]
    all_to_all x2 -> x1, blocking collectives: 15.3 us -> 41.2 us  [swap(): return lax.all_to_all(a, axis, split_axis=0, concat_axis=0, tiled=True)]
    all_to_all x2 -> x3, starting transfers between devices: 7.94 us -> 26.8 us  [swap(): return lax.all_to_all(a, axis, split_axis=0, concat_axis=0, tiled=True)]
  transfers between devices with their start and end apart: 6 -> 5, of which waited for: 5 -> 5; matrix products, arithmetic and copies ran while one was open for 2% -> 3% of each run, Pallas kernels for 0% -> 0%
where the time goes in v1:
time: 143 us
  waiting for transfers between devices  50.3 us (35%)
  blocking collectives  41.2 us (29%)
  starting transfers between devices  33.4 us (23%)
  local copies, waits for them, and re-layouts  7.9 us (6%)
  matrix products  5.56 us (4%)
  other arithmetic  3.7 us (3%)
    all_to_all x3, waiting for transfers between devices, swap(): return lax.all_to_all(a, axis, split_axis=0, concat_axis=0, tiled=True)  45.4 us
    all_to_all x1, blocking collectives, swap(): return lax.all_to_all(a, axis, split_axis=0, concat_axis=0, tiled=True)  41.2 us
    all_to_all x3, starting transfers between devices, swap(): return lax.all_to_all(a, axis, split_axis=0, concat_axis=0, tiled=True)  26.8 us
    ppermute x1, starting transfers between devices, on_device(): other = lax.ppermute(mine, 'core', [(0, 1), (1, 0)])  4.24 us
  transfers between devices with their start and end apart: 5, of which 5 were waited for; matrix products, arithmetic and copies ran while one was open for 3% of the time, Pallas kernels for 0%

profile of v1, /device:TPU:1, one launch (start us, length us, event | category | flops | bytes accessed | tf_op | source)
XLA Modules:
  0.0 142.9 jit_solution(14945011201512050793)
XLA Ops:
  0.6 0.0 copy-start
  0.6 0.9 stack.9
  1.5 0.8 stack.10
  2.3 0.6 broadcast_in_dim.79
  2.9 16.7 %all-to-all-start = ((bf16[24,8,128]{2,1,0:T(8,128)(2,1)}), bf16[24,8,128]{2,1,0:T(8,128)(2,1)S(1)}, u32[]{:S(2)}, u32[]{:S(2)}) async-start(bf16[24,8,128]{2,1,0:T(8,128)(2,1)} %bitcast.2), calls=%async_computation | async-start | bytes 98304 | tf_op jit(solution)/shard_map/all_to_all | solution.py:20
  19.6 0.7 fusion.22
  20.3 0.7 select_reduce_fusion.2
  21.1 0.1 select_reduce_fusion
  21.2 0.1 select_reduce_fusion.1
  21.3 0.1 mul.31
  21.4 8.3 %all-to-all-done = bf16[24,8,128]{2,1,0:T(8,128)(2,1)S(1)} async-done(((bf16[24,8,128]{2,1,0:T(8,128)(2,1)}), bf16[24,8,128]{2,1,0:T(8,128)(2,1)S(1)}, u32[]{:S(2)}, u32[]{:S(2)}) %all-to-all-start) | async-done | bytes 49184 | tf_op jit(solution)/shard_map/all_to_all | solution.py:20
  29.7 0.1 reshape.115
  29.9 0.1 copy.25
  29.9 0.1 reshape.116
  30.1 0.2 fusion.1
  30.3 0.1 broadcast_in_dim.83
  30.4 41.2 %all_to_all.20 = bf16[32,24,768]{2,1,0:T(8,128)(2,1)S(1)} all-to-all(bf16[32,24,768]{2,1,0:T(8,128)(2,1)S(1)} %bitcast.73), channel_id=1, replica_groups=mesh['y'=8,'z'=12,'core'=2,'expert'=4] {'y','expert'}, dimensions={0} | all-to-all | bytes 2359296 | tf_op jit(solution)/shard_map/all_to_all | solution.py:20
  71.6 0.1 copy.30
  71.7 0.0 copy-start.3
  71.7 4.2 %collective-permute-start = (bf16[96,6144]{1,0:T(8,128)(2,1)S(1)}, bf16[96,6144]{1,0:T(8,128)(2,1)S(1)}, u32[]{:S(2)}, u32[]{:S(2)}) collective-permute-start(bf16[96,6144]{1,0:T(8,128)(2,1)S(1)} %bitcast.67), channel_id=1, source_target_pairs={{0,4},{4,0},{1,5},{5,1},{2,6},{6,2},{3,7},{7,3},{8,12},{12,8},{9,1... | collective-permute-start | bytes 3538952 | tf_op jit(solution)/shard_map/ppermute | solution.py:56
  75.9 2.5 %collective-permute-done = bf16[96,6144]{1,0:T(8,128)(2,1)S(1)} collective-permute-done((bf16[96,6144]{1,0:T(8,128)(2,1)S(1)}, bf16[96,6144]{1,0:T(8,128)(2,1)S(1)}, u32[]{:S(2)}, u32[]{:S(2)}) %collective-permute-start) | collective-permute-done | bytes 1179680 | tf_op jit(solution)/shard_map/ppermute | solution.py:56
  78.4 0.0 copy-start.1
  78.4 0.1 broadcast_select_fusion.1
  78.5 0.0 copy-done.3
  78.5 0.0 copy-start.4
  78.5 0.5 fusion.12
  79.1 0.3 copy-done.1
  79.4 0.6 copy-done.4
  79.9 0.6 fusion.3
  80.5 0.0 copy-done
  80.5 0.6 multiply_convert_fusion.2
  81.1 0.5 fusion.5
  81.6 0.5 fusion.10
  82.0 0.6 select_convert_fusion
  82.6 2.3 %collective-permute-start.1 = (bf16[96,6144]{1,0:T(8,128)(2,1)S(1)}, bf16[96,6144]{1,0:T(8,128)(2,1)S(1)}, u32[]{:S(2)}, u32[]{:S(2)}) collective-permute-start(bf16[96,6144]{1,0:T(8,128)(2,1)S(1)} %get-tuple-element.14), channel_id=1, source_target_pairs={{0,4},{4,0},{1,5},{5,1},{2,6},{6,2},{3,7},{7,3},{8,12},{12,8},{9,1... | collective-permute-start | bytes 3538952 | tf_op jit(solution)/shard_map/ppermute | solution.py:75
  84.9 2.5 %collective-permute-done.1 = bf16[96,6144]{1,0:T(8,128)(2,1)S(1)} collective-permute-done((bf16[96,6144]{1,0:T(8,128)(2,1)S(1)}, bf16[96,6144]{1,0:T(8,128)(2,1)S(1)}, u32[]{:S(2)}, u32[]{:S(2)}) %collective-permute-start.1) | collective-permute-done | bytes 1179680 | tf_op jit(solution)/shard_map/ppermute | solution.py:75
  87.4 0.3 add_convert_fusion
  87.7 1.1 copy.33
  88.8 4.7 %all-to-all-start.2 = ((bf16[32,24,768]{2,1,0:T(8,128)(2,1)}), bf16[32,24,768]{2,1,0:T(8,128)(2,1)}, u32[]{:S(2)}, u32[]{:S(2)}) async-start(bf16[32,24,768]{2,1,0:T(8,128)(2,1)} %bitcast.72), calls=%async_computation.2 | async-start | bytes 2359296 | tf_op jit(solution)/shard_map/all_to_all | solution.py:20
  93.5 0.6 convolution_convert_fusion
  94.0 1.3 slice_bitcast_fusion
  95.3 28.3 %all-to-all-done.2 = bf16[32,24,768]{2,1,0:T(8,128)(2,1)} async-done(((bf16[32,24,768]{2,1,0:T(8,128)(2,1)}), bf16[32,24,768]{2,1,0:T(8,128)(2,1)}, u32[]{:S(2)}, u32[]{:S(2)}) %all-to-all-start.2) | async-done | bytes 1179680 | tf_op jit(solution)/shard_map/all_to_all | solution.py:20
  123.6 0.0 copy-start.2
  123.6 1.5 %convert_reduce_fusion = f32[4,24,768]{2,1,0:T(8,128)S(1)} fusion(bf16[8,4,24,768]{3,2,1,0:T(8,128)(2,1)} %bitcast.23), kind=kLoop, calls=%fused_computation.4 | loop fusion | flops 1105920 | bytes 1474560 | tf_op jit(solution)/shard_map/reduce_sum | solution.py:78
  125.2 0.3 fusion.2
  125.5 0.2 reshape.122
  125.7 0.8 reshape.123
  126.5 5.5 %all-to-all-start.3 = ((bf16[24,8,128]{2,1,0:T(8,128)(2,1)}), bf16[24,8,128]{2,1,0:T(8,128)(2,1)S(1)}, u32[]{:S(2)}, u32[]{:S(2)}) async-start(bf16[24,8,128]{2,1,0:T(8,128)(2,1)} %reshape.123), calls=%async_computation.3 | async-start | bytes 98304 | tf_op jit(solution)/shard_map/all_to_all | solution.py:20
  132.0 0.0 copy-done.2
  132.0 1.3 fusion
  133.3 8.8 %all-to-all-done.3 = bf16[24,8,128]{2,1,0:T(8,128)(2,1)S(1)} async-done(((bf16[24,8,128]{2,1,0:T(8,128)(2,1)}), bf16[24,8,128]{2,1,0:T(8,128)(2,1)S(1)}, u32[]{:S(2)}, u32[]{:S(2)}) %all-to-all-start.3) | async-done | bytes 49184 | tf_op jit(solution)/shard_map/all_to_all | solution.py:20
  142.1 0.1 reshape.124
  142.3 0.6 slice_bitcast_fusion.2
  (6 shorter events, 0.1 us)
Async XLA Ops:
  0.6 79.9 %copy-start = (bf16[1,64,6144]{2,1,0:T(8,128)(2,1)S(1)}, bf16[1,64,6144]{2,1,0:T(8,128)(2,1)}, u32[]{:S(2)}) copy-start(bf16[1,64,6144]{2,1,0:T(8,128)(2,1)} %param.11) | copy-start | bytes 2359300
  2.9 26.8 %all-to-all-start = ((bf16[24,8,128]{2,1,0:T(8,128)(2,1)}), bf16[24,8,128]{2,1,0:T(8,128)(2,1)S(1)}, u32[]{:S(2)}, u32[]{:S(2)}) async-start(bf16[24,8,128]{2,1,0:T(8,128)(2,1)} %bitcast.2), calls=%async_computation | async-start | bytes 98304 | tf_op jit(solution)/shard_map/all_to_all | solution.py:20
  71.7 6.8 %copy-start.3 = (bf16[1,64,6144]{2,1,0:T(8,128)(2,1)S(1)}, bf16[1,64,6144]{2,1,0:T(8,128)(2,1)}, u32[]{:S(2)}) copy-start(bf16[1,64,6144]{2,1,0:T(8,128)(2,1)} %param.10) | copy-start | bytes 2359300
  71.7 6.7 %collective-permute-start = (bf16[96,6144]{1,0:T(8,128)(2,1)S(1)}, bf16[96,6144]{1,0:T(8,128)(2,1)S(1)}, u32[]{:S(2)}, u32[]{:S(2)}) collective-permute-start(bf16[96,6144]{1,0:T(8,128)(2,1)S(1)} %bitcast.67), channel_id=1, source_target_pairs={{0,4},{4,0},{1,5},{5,1},{2,6},{6,2},{3,7},{7,3},{8,12},{12,8},{9,1... | collective-permute-start | bytes 3538952 | tf_op jit(solution)/shard_map/ppermute | solution.py:56
  78.4 1.0 copy-start.1
  78.5 1.4 %copy-start.4 = (bf16[1,64,6144]{2,1,0:T(8,128)(2,1)S(1)}, bf16[1,64,6144]{2,1,0:T(8,128)(2,1)}, u32[]{:S(2)}) copy-start(bf16[1,64,6144]{2,1,0:T(8,128)(2,1)} %param.12) | copy-start | bytes 2359300
  82.6 4.7 %collective-permute-start.1 = (bf16[96,6144]{1,0:T(8,128)(2,1)S(1)}, bf16[96,6144]{1,0:T(8,128)(2,1)S(1)}, u32[]{:S(2)}, u32[]{:S(2)}) collective-permute-start(bf16[96,6144]{1,0:T(8,128)(2,1)S(1)} %get-tuple-element.14), channel_id=1, source_target_pairs={{0,4},{4,0},{1,5},{5,1},{2,6},{6,2},{3,7},{7,3},{8,12},{12,8},{9,1... | collective-permute-start | bytes 3538952 | tf_op jit(solution)/shard_map/ppermute | solution.py:75
  88.8 34.8 %all-to-all-start.2 = ((bf16[32,24,768]{2,1,0:T(8,128)(2,1)}), bf16[32,24,768]{2,1,0:T(8,128)(2,1)}, u32[]{:S(2)}, u32[]{:S(2)}) async-start(bf16[32,24,768]{2,1,0:T(8,128)(2,1)} %bitcast.72), calls=%async_computation.2 | async-start | bytes 2359296 | tf_op jit(solution)/shard_map/all_to_all | solution.py:20
  123.6 8.4 %copy-start.2 = (bf16[96,6144]{1,0:T(8,128)(2,1)S(1)}, bf16[96,6144]{1,0:T(8,128)(2,1)}, u32[]{:S(2)}) copy-start(bf16[96,6144]{1,0:T(8,128)(2,1)} %copy-done.1) | copy-start | bytes 3538948
  126.5 15.6 %all-to-all-start.3 = ((bf16[24,8,128]{2,1,0:T(8,128)(2,1)}), bf16[24,8,128]{2,1,0:T(8,128)(2,1)S(1)}, u32[]{:S(2)}, u32[]{:S(2)}) async-start(bf16[24,8,128]{2,1,0:T(8,128)(2,1)} %reshape.123), calls=%async_computation.3 | async-start | bytes 98304 | tf_op jit(solution)/shard_map/all_to_all | solution.py:20

commit v2 on v1

v2 whole, which is shorter than its diff:
```python
import jax
import jax.numpy as jnp
from jax import lax
from jax.experimental import pallas as pl
from jax.experimental.pallas import tpu as pltpu
from jax.sharding import Mesh, PartitionSpec as P

CORES = 2
COLUMNS = 8
PAIR = 2
SLOTS = 24
HALF = 64
LANES = 128
ROOM = 40 * 1024 * 1024

bf16, f32 = jnp.bfloat16, jnp.float32


def tdot(a, b):
    return lax.dot_general(a, b, (((0,), (0,)), ((), ())), preferred_element_type=f32)


def ndot(a, b):
    return lax.dot_general(a, b, (((1,), (1,)), ((), ())), preferred_element_type=f32)


def swap(a, axis):
    return lax.all_to_all(a, axis, split_axis=0, concat_axis=0, tiled=True)


def across(a):
    return lax.ppermute(a, "core", [(0, 1), (1, 0)])


def cross(a, b):
    return (
        jnp.concatenate([a[:, :HALF], b[:, :HALF]], axis=1),
        jnp.concatenate([a[:, HALF:], b[:, HALF:]], axis=1),
    )


def tiles(width):
    per = width // (COLUMNS * 2 * LANES)
    for y in range(COLUMNS):
        for j in range(per):
            yield (y * per + j) * 2 * LANES, (y % PAIR) * PAIR, ((y // PAIR) * per + j) * LANES


def arrange(core_ref, gate_ref, up_ref, down_ref, keep_ref, send_ref):
    units = gate_ref.shape[0]

    def fill(pair_ref, single_ref):
        for at, place, to in tiles(gate_ref.shape[1]):
            a, b = slice(at, at + LANES), slice(at + LANES, at + 2 * LANES)
            for row, ref in ((0, gate_ref), (units, up_ref)):
                for zl, tile in enumerate(cross(ref[:, a], ref[:, b])):
                    pair_ref[place + zl, row:row + units, to:to + LANES] = tile
            for zl, tile in enumerate(cross(down_ref[:, a], down_ref[:, b])):
                single_ref[place + zl, 0:units, to:to + LANES] = tile
                single_ref[place + zl, units:2 * units, to:to + LANES] = tile

    @pl.when(core_ref[0] == 0)
    def _():
        fill(keep_ref, send_ref)

    @pl.when(core_ref[0] != 0)
    def _():
        fill(send_ref, keep_ref)


def project(mine_ref, keep_ref, recv_ref, out_ref):
    n = keep_ref.shape[1]
    for part, ref in ((0, keep_ref), (1, recv_ref)):
        total = ndot(mine_ref[0], ref[0])
        for b in range(1, mine_ref.shape[0]):
            total = total + ndot(mine_ref[b], ref[b])
        out_ref[:, part * n:(part + 1) * n] = total


def expand(core_ref, mine_ref, other_ref, keep_ref, recv_ref, part_ref, hidden_ref, pair_ref):
    units = hidden_ref.shape[1]
    first = core_ref[0] == 0
    mine, other = mine_ref[...], other_ref[...]
    own_front, far_front = mine[:, :2 * units], mine[:, 2 * units:]
    own_back, far_back = other[:, 2 * units:], other[:, :2 * units]
    sides = []
    for here, there in ((own_front, own_back), (far_front, far_back)):
        proj = jnp.where(first, here, there)
        dhid = jnp.where(first, there, here)[:, :units]
        gate, upper = proj[:, :units], proj[:, units:]
        sig = jax.nn.sigmoid(gate)
        act = gate * sig
        hidden = (act * upper).astype(bf16)
        dgate = (dhid * upper * sig * (1.0 + gate * (1.0 - sig))).astype(bf16)
        dup = (dhid * act).astype(bf16)
        sides.append((hidden, jnp.concatenate([dgate, dup], axis=1)))
    hidden_ref[...] = sides[0][0]
    pair_ref[...] = sides[0][1]
    lefts = []
    for hidden, pair in sides:
        lone = jnp.concatenate([hidden, jnp.zeros_like(hidden)], axis=1)
        lefts.append(jnp.where(first, pair.astype(f32), lone.astype(f32)).astype(bf16))
    for b in range(keep_ref.shape[0]):
        total = jnp.dot(lefts[0], keep_ref[b], preferred_element_type=f32)
        total = total + jnp.dot(lefts[1], recv_ref[b], preferred_element_type=f32)
        part_ref[b] = total.astype(bf16)


def weigh(core_ref, mine_ref, other_ref, hidden_ref, pair_ref, gate_ref, up_ref, down_ref):
    units = hidden_ref.shape[1]

    def fill(rows_ref, cot_ref):
        hidden, pair = hidden_ref[...], pair_ref[...]
        for at, place, to in tiles(gate_ref.shape[1]):
            both = []
            for ref in (rows_ref, cot_ref):
                both.append(jnp.concatenate(cross(ref[place, :, to:to + LANES], ref[place + 1, :, to:to + LANES]), axis=1))
            grads = tdot(pair, both[0]).astype(bf16)
            gate_ref[:, at:at + 2 * LANES] = grads[:units]
            up_ref[:, at:at + 2 * LANES] = grads[units:]
            down_ref[:, at:at + 2 * LANES] = tdot(hidden, both[1]).astype(bf16)

    @pl.when(core_ref[0] == 0)
    def _():
        fill(mine_ref, other_ref)

    @pl.when(core_ref[0] != 0)
    def _():
        fill(other_ref, mine_ref)


def kernel(body, outs, cost, core, *arrays):
    specs = [pl.BlockSpec(memory_space=pltpu.VMEM)] * len(arrays)
    if core is not None:
        specs, arrays = [pl.BlockSpec(memory_space=pltpu.SMEM)] + specs, (core,) + arrays
    return pl.pallas_call(
        body,
        out_shape=tuple(jax.ShapeDtypeStruct(s, d) for s, d in outs),
        in_specs=specs,
        out_specs=tuple(pl.BlockSpec(memory_space=pltpu.VMEM) for _ in outs),
        compiler_params=pltpu.CompilerParams(vmem_limit_bytes=ROOM),
        cost_estimate=pl.CostEstimate(flops=cost[0], bytes_accessed=cost[1], transcendentals=0),
        name=body.__name__,
    )(*arrays)


def on_device(tokens, routes, probs, w_gate, w_up, w_down, grad_out):
    experts = lax.axis_size("expert")
    cells = lax.axis_size("yh") * lax.axis_size("zh")
    near = PAIR * PAIR
    core = lax.axis_index("core")
    first = core == 0
    flag = core.astype(jnp.int32).reshape(1)
    count, narrow = tokens.shape
    wide = cells * CORES * narrow
    rows_of = experts * SLOTS
    units, width = w_gate.shape[1:]

    labels = lax.broadcasted_iota(jnp.int32, (experts, count, routes.shape[1]), 0)
    hits = routes[None] == labels
    mask = jnp.any(hits, axis=2)
    share = jnp.sum(jnp.where(hits, probs[None], 0.0), axis=2)
    earlier = lax.broadcasted_iota(jnp.int32, (count, count), 1) < lax.broadcasted_iota(jnp.int32, (count, count), 0)
    place = jnp.sum(jnp.where(earlier[None] & mask[:, None, :], 1, 0), axis=2)
    slots = lax.broadcasted_iota(jnp.int32, (experts, SLOTS, count), 1)
    chosen = (place[:, None, :] == slots) & mask[:, None, :]
    pick = chosen.reshape(rows_of, count).astype(bf16)
    weight = jnp.where(first, jnp.ones_like(share), share)
    slot_weight = jnp.sum(jnp.where(chosen, weight[:, None, :], 0.0), axis=2).reshape(rows_of, 1)

    both = jnp.stack([tokens, grad_out]).reshape(1, CORES, count * narrow // LANES, LANES)
    sent = jnp.broadcast_to(both, (cells,) + both.shape[1:]).reshape(cells * CORES, -1, LANES)
    got = swap(sent, ("yh", "zh", "core")).reshape(cells * CORES, count, narrow)
    local = got.transpose(1, 0, 2).reshape(count, wide)

    big = 2 * units * width
    keep, send = kernel(
        arrange, [((near, 2 * units, wide), bf16)] * 2, (0, 8 * big), flag, w_gate[0], w_up[0], w_down[0]
    )
    recv = across(send)

    packed = (jnp.dot(pick, local, preferred_element_type=f32) * slot_weight).astype(bf16)
    sent = jnp.broadcast_to(packed.reshape(1, experts, SLOTS, wide), (near, experts, SLOTS, wide))
    got = swap(sent.reshape(near * experts, SLOTS, wide), ("yl", "zl", "expert"))
    mine = got.reshape(near, rows_of, wide)

    work = 2 * rows_of * 2 * big
    (proj,) = kernel(project, [((rows_of, 4 * units), f32)], (work, 6 * big), None, mine, keep, recv)
    part, hidden, pair = kernel(
        expand,
        [((near, rows_of, wide), bf16), ((rows_of, units), bf16), ((rows_of, 2 * units), bf16)],
        (work, 6 * big), flag, proj, across(proj), keep, recv,
    )

    got = swap(part.reshape(near * experts, SLOTS, wide), ("yl", "zl", "expert"))
    summed = jnp.sum(got.reshape(near, rows_of, wide).astype(f32), axis=0)
    back_weight = jnp.where(first, mask.astype(f32), share)
    spread = jnp.where(chosen, back_weight[:, None, :], 0.0).reshape(rows_of, count)
    placed = lax.dot_general(
        spread, summed, (((0,), (0,)), ((), ())), precision=lax.Precision.HIGHEST, preferred_element_type=f32
    ).astype(bf16)
    sent = placed.reshape(count, cells * CORES, narrow).transpose(1, 0, 2).reshape(cells * CORES, -1, LANES)
    got = swap(sent, ("yh", "zh", "core")).reshape(cells, CORES, count, narrow)
    result = jnp.sum(got.astype(f32), axis=0).astype(bf16)

    mine, part = lax.optimization_barrier((mine, part))
    grad_gate, grad_up, grad_down = kernel(
        weigh, [((units, width), bf16)] * 3, (work, 8 * big), flag, mine, across(mine), hidden, pair
    )
    return (result[1], result[0], grad_gate[None], grad_up[None], grad_down[None])


def solution(mesh):
    dp, experts = mesh.devices.shape
    depth = dp // (COLUMNS * CORES)
    split = mesh.devices.reshape(COLUMNS // PAIR, PAIR, depth // PAIR, PAIR, CORES, experts)
    fine = Mesh(split, ("yh", "yl", "zh", "zl", "core", "expert"))
    dp = ("yh", "yl", "zh", "zl", "core")
    placed = (
        P("expert", dp),
        P("expert", None),
        P("expert", None),
        P("expert", dp, None),
        P("expert", dp, None),
        P("expert", dp, None),
        P("expert", dp),
    )
    return jax.shard_map(
        on_device,
        mesh=fine,
        in_specs=placed,
        out_specs=(P("expert", dp), P("expert", dp), P("expert", dp, None), P("expert", dp, None), P("expert", dp, None)),
        check_vma=False,
    )
```

time: 143 us -> 122 us (0.85)
  blocking collectives: 41.2 us -> 0 us
  starting transfers between devices: 33.4 us -> 44.4 us
  Pallas kernels: 0 us -> 4.93 us
  matrix products: 5.56 us -> 0.64 us
  waiting for transfers between devices: 50.3 us -> 55 us
  local copies, waits for them, and re-layouts: 7.9 us -> 12 us
    all_to_all x1 -> x0, blocking collectives: 41.2 us -> none  [swap(): return lax.all_to_all(a, axis, split_axis=0, concat_axis=0, tiled=True)]
    all_to_all x3 -> x4, starting transfers between devices: 26.8 us -> 36.2 us  [swap(): return lax.all_to_all(a, axis, split_axis=0, concat_axis=0, tiled=True)]
    all_to_all x3 -> x4, waiting for transfers between devices: 45.4 us -> 51 us  [swap(): return lax.all_to_all(a, axis, split_axis=0, concat_axis=0, tiled=True)]
    unnamed x10 -> x14, local copies, waits for them, and re-layouts: 0.89 us -> 5.86 us
    pallas_call x0 -> x4, Pallas kernels: none -> 4.93 us  [kernel(): pl.pallas_call(body, out_shape=tuple((jax.ShapeDtypeStruct(s, d) for s, d...]
    dot_general x10 -> x2, matrix products: 5.56 us -> 0.64 us  [the longest x1 0.43 us: on_device(): lax.dot_general(spread, summed, (((0,), (0,)), ((), ())), precision=lax.P...]
    ppermute x2 -> x3, starting transfers between devices: 6.52 us -> 8.26 us  [across(): return lax.ppermute(a, 'core', [(0, 1), (1, 0)])]
    ppermute x2 -> x3, waiting for transfers between devices: 4.91 us -> 3.94 us  [across(): return lax.ppermute(a, 'core', [(0, 1), (1, 0)])]
  transfers between devices with their start and end apart: 5 -> 7, of which waited for: 5 -> 6; matrix products, arithmetic and copies ran while one was open for 3% -> 4% of each run, Pallas kernels for 0% -> 2%
where the time goes in v2:
time: 122 us; the launch traced here: 121 us
  waiting for transfers between devices  55 us (45%)
  starting transfers between devices  44.4 us (36%)
  local copies, waits for them, and re-layouts  12 us (10%)
  Pallas kernels  4.93 us (4%)
  other arithmetic  3.35 us (3%)
    all_to_all x4, waiting for transfers between devices, swap(): return lax.all_to_all(a, axis, split_axis=0, concat_axis=0, tiled=True)  51 us
    all_to_all x4, starting transfers between devices, swap(): return lax.all_to_all(a, axis, split_axis=0, concat_axis=0, tiled=True)  36.2 us
    ppermute x3, starting transfers between devices, across(): return lax.ppermute(a, 'core', [(0, 1), (1, 0)])  8.26 us
    unnamed x14, local copies, waits for them, and re-layouts  5.86 us
    pallas_call x4, Pallas kernels, kernel(): pl.pallas_call(body, out_shape=tuple((jax.ShapeDtypeStruct(s, d) for s, d...  4.93 us
    ppermute x3, waiting for transfers between devices, across(): return lax.ppermute(a, 'core', [(0, 1), (1, 0)])  3.94 us
  transfers between devices with their start and end apart: 7, of which 6 were waited for; matrix products, arithmetic and copies ran while one was open for 4% of the time, Pallas kernels for 2%

profile of v2, /device:TPU:1, one launch (start us, length us, event | category | flops | bytes accessed | tf_op | source)
XLA Modules:
  0.0 121.1 jit_solution(8682065960163335906)
XLA Ops:
  0.6 0.8 stack.10
  1.4 0.8 stack.9
  2.2 0.7 broadcast_in_dim.84
  2.9 21.6 %all-to-all-start = ((bf16[48,8,128]{2,1,0:T(8,128)(2,1)}), bf16[48,8,128]{2,1,0:T(8,128)(2,1)S(1)}, u32[]{:S(2)}, u32[]{:S(2)}) async-start(bf16[48,8,128]{2,1,0:T(8,128)(2,1)} %bitcast.6), calls=%async_computation | async-start | bytes 196608 | tf_op jit(solution)/shard_map/all_to_all | solution.py:28
  24.5 0.7 fusion.3
  25.2 0.7 select_reduce_fusion.2
  25.9 0.1 select_reduce_fusion
  26.1 0.1 select_reduce_fusion.1
  26.2 0.1 mul.10
  26.3 14.5 %all-to-all-done = bf16[48,8,128]{2,1,0:T(8,128)(2,1)S(1)} async-done(((bf16[48,8,128]{2,1,0:T(8,128)(2,1)}), bf16[48,8,128]{2,1,0:T(8,128)(2,1)S(1)}, u32[]{:S(2)}, u32[]{:S(2)}) %all-to-all-start) | async-done | bytes 98336 | tf_op jit(solution)/shard_map/all_to_all | solution.py:28
  40.8 0.2 reshape.116
  41.0 0.2 copy.18
  41.2 0.3 reshape.117
  41.5 0.2 fusion
  41.7 1.1 broadcast_in_dim.89
  42.8 0.0 copy-start.4
  42.8 4.6 %all-to-all-start.1 = ((bf16[16,24,1536]{2,1,0:T(8,128)(2,1)}), bf16[16,24,1536]{2,1,0:T(8,128)(2,1)S(1)}, u32[]{:S(2)}, u32[]{:S(2)}) async-start(bf16[16,24,1536]{2,1,0:T(8,128)(2,1)} %bitcast.9), calls=%async_computation.1 | async-start | bytes 2359296 | tf_op jit(solution)/shard_map/all_to_all | solution.py:28
  47.5 0.0 copy-done.4
  47.5 0.0 copy-start.5
  47.5 1.1 copy-done.5
  48.6 0.0 copy-start.6
  48.6 1.1 copy-done.6
  49.7 0.7 arrange.1
  50.4 2.6 %collective-permute-start = (bf16[4,128,1536]{2,1,0:T(8,128)(2,1)S(1)}, bf16[4,128,1536]{2,1,0:T(8,128)(2,1)S(1)}, u32[]{:S(2)}, u32[]{:S(2)}) collective-permute-start(bf16[4,128,1536]{2,1,0:T(8,128)(2,1)S(1)} %get-tuple-element.15), channel_id=1, source_target_pairs={{0,4},{4,0},{1,5},{5,1},{2,6},{6,2},{3,7},{7,3},{8,12},{12,8},{9,1... | collective-permute-start | bytes 4718600 | tf_op jit(solution)/shard_map/ppermute | solution.py:32
  53.0 3.0 %collective-permute-done.recv_ref = bf16[4,128,1536]{2,1,0:T(8,128)(2,1)S(1)} collective-permute-done((bf16[4,128,1536]{2,1,0:T(8,128)(2,1)S(1)}, bf16[4,128,1536]{2,1,0:T(8,128)(2,1)S(1)}, u32[]{:S(2)}, u32[]{:S(2)}) %collective-permute-start) | collective-permute-done | bytes 1572896 | tf_op jit(solution)/shard_map/ppermute | solution.py:32
  56.1 0.0 copy-start
  56.1 1.2 copy-done
  57.2 8.0 %all-to-all-done.1 = bf16[16,24,1536]{2,1,0:T(8,128)(2,1)S(1)} async-done(((bf16[16,24,1536]{2,1,0:T(8,128)(2,1)}), bf16[16,24,1536]{2,1,0:T(8,128)(2,1)S(1)}, u32[]{:S(2)}, u32[]{:S(2)}) %all-to-all-start.1) | async-done | bytes 1179680 | tf_op jit(solution)/shard_map/all_to_all | solution.py:28
  65.2 0.0 copy-start.1
  65.2 1.4 %copy-done.1 = bf16[4,128,1536]{2,1,0:T(8,128)(2,1)S(1)} copy-done((bf16[4,128,1536]{2,1,0:T(8,128)(2,1)S(1)}, bf16[4,128,1536]{2,1,0:T(8,128)(2,1)}, u32[]{:S(2)}) %copy-start.1) | copy-done | bytes 1572888
  66.6 0.0 copy-start.2
  66.6 1.1 project.1.mine_ref
  67.7 3.4 %collective-permute-start.1 = (f32[96,256]{1,0:T(8,128)S(1)}, f32[96,256]{1,0:T(8,128)S(1)}, u32[]{:S(2)}, u32[]{:S(2)}) collective-permute-start(f32[96,256]{1,0:T(8,128)S(1)} %project.1.mine_ref), channel_id=1, source_target_pairs={{0,4},{4,0},{1,5},{5,1},{2,6},{6,2},{3,7},{7,3},{8,12},{12,8},{9,1... | collective-permute-start | bytes 294920 | tf_op jit(solution)/shard_map/ppermute | solution.py:32
  71.1 0.9 collective-permute-done.1.other_ref
  72.0 0.0 copy-done.2
  72.0 0.8 expand.1
  72.9 0.0 copy-start.3
  72.9 1.0 copy-done.3
  73.9 4.4 %all-to-all-start.2 = ((bf16[16,24,1536]{2,1,0:T(8,128)(2,1)}), bf16[16,24,1536]{2,1,0:T(8,128)(2,1)}, u32[]{:S(2)}, u32[]{:S(2)}) async-start(bf16[16,24,1536]{2,1,0:T(8,128)(2,1)} %bitcast.42), calls=%async_computation.2 | async-start | bytes 2359296 | tf_op jit(solution)/shard_map/all_to_all | solution.py:28
  78.3 2.3 %collective-permute-start.2 = (bf16[4,96,1536]{2,1,0:T(8,128)(2,1)S(1)}, bf16[4,96,1536]{2,1,0:T(8,128)(2,1)S(1)}, u32[]{:S(2)}, u32[]{:S(2)}) collective-permute-start(bf16[4,96,1536]{2,1,0:T(8,128)(2,1)S(1)} %bitcast.40), channel_id=1, source_target_pairs={{0,4},{4,0},{1,5},{5,1},{2,6},{6,2},{3,7},{7,3},{8,12},{12,8},{9,1... | collective-permute-start | bytes 3538952 | tf_op jit(solution)/shard_map/ppermute | solution.py:32
  80.6 0.1 iota.48
  80.7 0.1 bitcast_select_fusion
  80.8 15.3 %all-to-all-done.2 = bf16[16,24,1536]{2,1,0:T(8,128)(2,1)} async-done(((bf16[16,24,1536]{2,1,0:T(8,128)(2,1)}), bf16[16,24,1536]{2,1,0:T(8,128)(2,1)}, u32[]{:S(2)}, u32[]{:S(2)}) %all-to-all-start.2) | async-done | bytes 1179680 | tf_op jit(solution)/shard_map/all_to_all | solution.py:28
  96.1 1.5 %convert_reduce_fusion = f32[96,1536]{1,0:T(8,128)S(1)} fusion(bf16[4,96,1536]{2,1,0:T(8,128)(2,1)} %bitcast.38), kind=kLoop, calls=%fused_computation.1 | loop fusion | flops 1032192 | bytes 1769472 | tf_op jit(solution)/shard_map/reduce_sum | solution.py:196
  97.6 0.4 convolution_convert_fusion
  98.0 0.2 reshape.121
  98.3 0.1 copy.19
  98.4 0.9 reshape.122
  99.2 5.5 %all-to-all-start.3 = ((bf16[48,8,128]{2,1,0:T(8,128)(2,1)}), bf16[48,8,128]{2,1,0:T(8,128)(2,1)S(1)}, u32[]{:S(2)}, u32[]{:S(2)}) async-start(bf16[48,8,128]{2,1,0:T(8,128)(2,1)} %reshape.122), calls=%async_computation.3 | async-start | bytes 196608 | tf_op jit(solution)/shard_map/all_to_all | solution.py:28
  104.8 0.0 collective-permute-done.2.other_ref
  104.8 2.3 %weigh.1 = (bf16[64,6144]{1,0:T(8,128)(2,1)}, bf16[64,6144]{1,0:T(8,128)(2,1)}, bf16[64,6144]{1,0:T(8,128)(2,1)}) custom-call(s32[1]{0:T(128)} %bitcast.3.core_ref, bf16[4,96,1536]{2,1,0:T(8,128)(2,1)S(1)} %bitcast.41, bf16[4,96,1536]{2,1,0:T(8,128)(2,1)S(1)} %collective-permute-done.2.other_ref, bf16[96,64]{1,0:T(8,128)(2,1)S(1)} %get-tuple-element.18.hidden_ref, ...), custom_call_target="tpu_custom_call" | custom-call | flops 301989888 | bytes 6291456 | tf_op jit(solution)/shard_map/weigh/pallas_call | solution.py:136
  107.1 13.1 %all-to-all-done.3 = bf16[48,8,128]{2,1,0:T(8,128)(2,1)S(1)} async-done(((bf16[48,8,128]{2,1,0:T(8,128)(2,1)}), bf16[48,8,128]{2,1,0:T(8,128)(2,1)S(1)}, u32[]{:S(2)}, u32[]{:S(2)}) %all-to-all-start.3) | async-done | bytes 98336 | tf_op jit(solution)/shard_map/all_to_all | solution.py:28
  120.2 0.2 reshape.123
  120.4 0.1 reduce_sum.52
  120.5 0.6 slice_bitcast_fusion
  (5 shorter events, 0.0 us)
Async XLA Ops:
  2.9 38.0 %all-to-all-start = ((bf16[48,8,128]{2,1,0:T(8,128)(2,1)}), bf16[48,8,128]{2,1,0:T(8,128)(2,1)S(1)}, u32[]{:S(2)}, u32[]{:S(2)}) async-start(bf16[48,8,128]{2,1,0:T(8,128)(2,1)} %bitcast.6), calls=%async_computation | async-start | bytes 196608 | tf_op jit(solution)/shard_map/all_to_all | solution.py:28
  42.8 4.6 %copy-start.4 = (bf16[1,64,6144]{2,1,0:T(8,128)(2,1)S(1)}, bf16[1,64,6144]{2,1,0:T(8,128)(2,1)}, u32[]{:S(2)}) copy-start(bf16[1,64,6144]{2,1,0:T(8,128)(2,1)} %param.10) | copy-start | bytes 2359300
  42.8 22.3 %all-to-all-start.1 = ((bf16[16,24,1536]{2,1,0:T(8,128)(2,1)}), bf16[16,24,1536]{2,1,0:T(8,128)(2,1)S(1)}, u32[]{:S(2)}, u32[]{:S(2)}) async-start(bf16[16,24,1536]{2,1,0:T(8,128)(2,1)} %bitcast.9), calls=%async_computation.1 | async-start | bytes 2359296 | tf_op jit(solution)/shard_map/all_to_all | solution.py:28
  47.5 1.1 copy-start.5
  48.6 1.1 copy-start.6
  50.4 5.6 %collective-permute-start = (bf16[4,128,1536]{2,1,0:T(8,128)(2,1)S(1)}, bf16[4,128,1536]{2,1,0:T(8,128)(2,1)S(1)}, u32[]{:S(2)}, u32[]{:S(2)}) collective-permute-start(bf16[4,128,1536]{2,1,0:T(8,128)(2,1)S(1)} %get-tuple-element.15), channel_id=1, source_target_pairs={{0,4},{4,0},{1,5},{5,1},{2,6},{6,2},{3,7},{7,3},{8,12},{12,8},{9,1... | collective-permute-start | bytes 4718600 | tf_op jit(solution)/shard_map/ppermute | solution.py:32
  56.1 1.2 copy-start
  65.2 1.4 %copy-start.1 = (bf16[4,128,1536]{2,1,0:T(8,128)(2,1)S(1)}, bf16[4,128,1536]{2,1,0:T(8,128)(2,1)}, u32[]{:S(2)}) copy-start(bf16[4,128,1536]{2,1,0:T(8,128)(2,1)} %copy-done) | copy-start | bytes 4718596
  66.6 5.4 %copy-start.2 = (bf16[4,128,1536]{2,1,0:T(8,128)(2,1)S(1)}, bf16[4,128,1536]{2,1,0:T(8,128)(2,1)}, u32[]{:S(2)}) copy-start(bf16[4,128,1536]{2,1,0:T(8,128)(2,1)} %copy-done) | copy-start | bytes 4718596
  67.7 4.3 %collective-permute-start.1 = (f32[96,256]{1,0:T(8,128)S(1)}, f32[96,256]{1,0:T(8,128)S(1)}, u32[]{:S(2)}, u32[]{:S(2)}) collective-permute-start(f32[96,256]{1,0:T(8,128)S(1)} %project.1.mine_ref), channel_id=1, source_target_pairs={{0,4},{4,0},{1,5},{5,1},{2,6},{6,2},{3,7},{7,3},{8,12},{12,8},{9,1... | collective-permute-start | bytes 294920 | tf_op jit(solution)/shard_map/ppermute | solution.py:32
  72.9 1.0 copy-start.3
  73.9 22.2 %all-to-all-start.2 = ((bf16[16,24,1536]{2,1,0:T(8,128)(2,1)}), bf16[16,24,1536]{2,1,0:T(8,128)(2,1)}, u32[]{:S(2)}, u32[]{:S(2)}) async-start(bf16[16,24,1536]{2,1,0:T(8,128)(2,1)} %bitcast.42), calls=%async_computation.2 | async-start | bytes 2359296 | tf_op jit(solution)/shard_map/all_to_all | solution.py:28
  78.3 26.5 %collective-permute-start.2 = (bf16[4,96,1536]{2,1,0:T(8,128)(2,1)S(1)}, bf16[4,96,1536]{2,1,0:T(8,128)(2,1)S(1)}, u32[]{:S(2)}, u32[]{:S(2)}) collective-permute-start(bf16[4,96,1536]{2,1,0:T(8,128)(2,1)S(1)} %bitcast.40), channel_id=1, source_target_pairs={{0,4},{4,0},{1,5},{5,1},{2,6},{6,2},{3,7},{7,3},{8,12},{12,8},{9,1... | collective-permute-start | bytes 3538952 | tf_op jit(solution)/shard_map/ppermute | solution.py:32
  99.2 21.0 %all-to-all-start.3 = ((bf16[48,8,128]{2,1,0:T(8,128)(2,1)}), bf16[48,8,128]{2,1,0:T(8,128)(2,1)S(1)}, u32[]{:S(2)}, u32[]{:S(2)}) async-start(bf16[48,8,128]{2,1,0:T(8,128)(2,1)} %reshape.122), calls=%async_computation.3 | async-start | bytes 196608 | tf_op jit(solution)/shard_map/all_to_all | solution.py:28

commit v3 on v2

v3 whole, which is shorter than its diff:
```python
import jax
import jax.numpy as jnp
from jax import lax
from jax.experimental import pallas as pl
from jax.experimental.pallas import tpu as pltpu
from jax.sharding import Mesh, PartitionSpec as P

CORES = 2
COLUMNS = 8
PAIR = 2
SLOTS = 24
HALF = 64
LANES = 128
ROOM = 16 * 1024 * 1024
ALL = 60 * 1024 * 1024

bf16, f32 = jnp.bfloat16, jnp.float32


def tdot(a, b):
    return lax.dot_general(a, b, (((0,), (0,)), ((), ())), preferred_element_type=f32)


def ndot(a, b):
    return lax.dot_general(a, b, (((1,), (1,)), ((), ())), preferred_element_type=f32)


def swap(a, axis):
    return lax.all_to_all(a, axis, split_axis=0, concat_axis=0, tiled=True)


def across(a):
    return lax.ppermute(a, "core", [(0, 1), (1, 0)])


def cross(a, b):
    return (
        jnp.concatenate([a[:, :HALF], b[:, :HALF]], axis=1),
        jnp.concatenate([a[:, HALF:], b[:, HALF:]], axis=1),
    )


def tiles(width):
    per = width // (COLUMNS * 2 * LANES)
    for y in range(COLUMNS):
        for j in range(per):
            yield (y * per + j) * 2 * LANES, (y % PAIR) * PAIR, ((y // PAIR) * per + j) * LANES


def arrange(core_ref, gate_ref, up_ref, down_ref, keep_ref, send_ref):
    units = gate_ref.shape[0]

    def fill(pair_ref, single_ref):
        for at, place, to in tiles(gate_ref.shape[1]):
            a, b = slice(at, at + LANES), slice(at + LANES, at + 2 * LANES)
            for row, ref in ((0, gate_ref), (units, up_ref)):
                for zl, tile in enumerate(cross(ref[:, a], ref[:, b])):
                    pair_ref[place + zl, row:row + units, to:to + LANES] = tile
            for zl, tile in enumerate(cross(down_ref[:, a], down_ref[:, b])):
                single_ref[place + zl, 0:units, to:to + LANES] = tile
                single_ref[place + zl, units:2 * units, to:to + LANES] = tile

    @pl.when(core_ref[0] == 0)
    def _():
        fill(keep_ref, send_ref)

    @pl.when(core_ref[0] != 0)
    def _():
        fill(send_ref, keep_ref)


def join(keep_ref, recv_ref, out_ref):
    n = keep_ref.shape[1]
    for b in range(keep_ref.shape[0]):
        out_ref[b, :n] = keep_ref[b]
        out_ref[b, n:] = recv_ref[b]


def project(mine_ref, weights_ref, out_ref):
    n = weights_ref.shape[1] // 2
    for at in (0, n):
        total = ndot(mine_ref[0], weights_ref[0, at:at + n])
        for b in range(1, mine_ref.shape[0]):
            total = total + ndot(mine_ref[b], weights_ref[b, at:at + n])
        out_ref[:, at:at + n] = total


def activate(proj, dhid):
    units = dhid.shape[1]
    gate, upper = proj[:, :units], proj[:, units:]
    sig = jax.nn.sigmoid(gate)
    act = gate * sig
    hidden = (act * upper).astype(bf16)
    dgate = (dhid * upper * sig * (1.0 + gate * (1.0 - sig))).astype(bf16)
    dup = (dhid * act).astype(bf16)
    return hidden, jnp.concatenate([dgate, dup], axis=1)


def expand(core_ref, mine_ref, other_ref, weights_ref, part_ref):
    half = mine_ref.shape[1] // 2
    first = core_ref[0] == 0
    lefts = []
    for own, far in ((slice(0, half), slice(half, 2 * half)), (slice(half, 2 * half), slice(0, half))):
        here, there = mine_ref[:, own], other_ref[:, far]
        hidden, pair = activate(jnp.where(first, here, there), jnp.where(first, there, here)[:, :half // 2])
        lone = jnp.concatenate([hidden, jnp.zeros_like(hidden)], axis=1)
        lefts.append(jnp.where(first, pair.astype(f32), lone.astype(f32)).astype(bf16))
    left = jnp.concatenate(lefts, axis=1)
    for b in range(weights_ref.shape[0]):
        part_ref[b] = jnp.dot(left, weights_ref[b], preferred_element_type=f32).astype(bf16)


def weigh(core_ref, mine_ref, other_ref, here_ref, there_ref, gate_ref, up_ref, down_ref):
    units = gate_ref.shape[0]
    half = 2 * units

    def fill(rows_ref, cot_ref, proj, dhid):
        hidden, pair = activate(proj, dhid[:, :units])
        for at, place, to in tiles(gate_ref.shape[1]):
            both = []
            for ref in (rows_ref, cot_ref):
                both.append(jnp.concatenate(cross(ref[place, :, to:to + LANES], ref[place + 1, :, to:to + LANES]), axis=1))
            grads = tdot(pair, both[0]).astype(bf16)
            gate_ref[:, at:at + 2 * LANES] = grads[:units]
            up_ref[:, at:at + 2 * LANES] = grads[units:]
            down_ref[:, at:at + 2 * LANES] = tdot(hidden, both[1]).astype(bf16)

    here, there = here_ref[:, :half], there_ref[:, half:]

    @pl.when(core_ref[0] == 0)
    def _():
        fill(mine_ref, other_ref, here, there)

    @pl.when(core_ref[0] != 0)
    def _():
        fill(other_ref, mine_ref, there, here)


def turn(parts):
    n = len(parts)
    size = LANES // n
    group = lax.broadcasted_iota(jnp.int32, parts[0].shape, 1) // size
    outs = []
    for s in range(n):
        total = parts[s]
        for q in range(n):
            if q != s:
                total = jnp.where(group == q, pltpu.roll(parts[q], size * ((q - s) % n), 1), total)
        outs.append(total)
    return outs


def fan(tokens_ref, grad_ref, out_ref, both_ref, sem):
    copies = []
    for array, ref in enumerate((tokens_ref, grad_ref)):
        copies.append(pltpu.make_async_copy(ref, both_ref.at[array], sem.at[array]))
        copies[-1].start()
    for array, copy in enumerate(copies):
        copy.wait()
        rows = both_ref[array].astype(f32)
        lines = rows.shape[0] * rows.shape[1] // LANES
        pieces = [rows[at:at + lines] for at in range(0, rows.shape[0], lines)]
        packed = jnp.concatenate(pieces, axis=1).astype(bf16)
        for cell in range(out_ref.shape[0] // CORES):
            out_ref[cell * CORES + array] = packed


def dispatch(got_ref, pick_ref, weight_ref, out_ref):
    count = pick_ref.shape[1]
    lines = got_ref.shape[1]
    n = count // lines
    columns = []
    for g in range(got_ref.shape[0] // n):
        columns.append(jnp.concatenate(turn([got_ref[g * n + s].astype(f32) for s in range(n)]), axis=0))
    local = jnp.concatenate(columns, axis=1).astype(bf16)
    packed = jnp.dot(pick_ref[...], local, preferred_element_type=f32) * weight_ref[...]
    experts = pick_ref.shape[0] // SLOTS
    for e in range(experts):
        rows = packed[e * SLOTS:(e + 1) * SLOTS].astype(bf16)
        for b in range(out_ref.shape[0] // experts):
            out_ref[b * experts + e] = rows


def combine(got_ref, spread_ref, out_ref):
    experts = spread_ref.shape[1] // SLOTS
    sums = []
    for e in range(experts):
        total = got_ref[e].astype(f32)
        for b in range(1, got_ref.shape[0] // experts):
            total = total + got_ref[b * experts + e].astype(f32)
        sums.append(total)
    placed = lax.dot_general(
        spread_ref[...], jnp.concatenate(sums, axis=0), (((1,), (0,)), ((), ())),
        precision=lax.Precision.HIGHEST, preferred_element_type=f32,
    )
    lines = out_ref.shape[1]
    n = placed.shape[0] // lines
    for g in range(out_ref.shape[0] // n):
        column = placed[:, g * LANES:(g + 1) * LANES]
        for s, line in enumerate(turn([column[q * lines:(q + 1) * lines] for q in range(n)])):
            out_ref[g * n + s] = line.astype(bf16)


def finish(got_ref, back_ref, out_ref):
    for array, ref in enumerate((back_ref, out_ref)):
        total = got_ref[array].astype(f32)
        for cell in range(1, got_ref.shape[0] // CORES):
            total = total + got_ref[cell * CORES + array].astype(f32)
        narrow = ref.shape[1]
        pieces = [total[:, at:at + narrow] for at in range(0, LANES, narrow)]
        ref[...] = jnp.concatenate(pieces, axis=0).astype(bf16)


def kernel(body, outs, cost, core, *arrays, places=pltpu.VMEM, scratch=(), room=ROOM):
    specs = [pl.BlockSpec(memory_space=places)] * len(arrays)
    if core is not None:
        specs, arrays = [pl.BlockSpec(memory_space=pltpu.SMEM)] + specs, (core,) + arrays
    return pl.pallas_call(
        body,
        out_shape=tuple(jax.ShapeDtypeStruct(s, d) for s, d in outs),
        in_specs=specs,
        out_specs=tuple(pl.BlockSpec(memory_space=pltpu.VMEM) for _ in outs),
        scratch_shapes=list(scratch),
        compiler_params=pltpu.CompilerParams(vmem_limit_bytes=room),
        cost_estimate=pl.CostEstimate(flops=cost[0], bytes_accessed=cost[1], transcendentals=0),
        name=body.__name__,
    )(*arrays)


def on_device(tokens, routes, probs, w_gate, w_up, w_down, grad_out):
    experts = lax.axis_size("expert")
    cells = lax.axis_size("yh") * lax.axis_size("zh")
    near = PAIR * PAIR
    core = lax.axis_index("core")
    first = core == 0
    flag = core.astype(jnp.int32).reshape(1)
    count, narrow = tokens.shape
    wide = cells * CORES * narrow
    rows_of = experts * SLOTS
    units, width = w_gate.shape[1:]

    labels = lax.broadcasted_iota(jnp.int32, (experts, count, routes.shape[1]), 0)
    hits = routes[None] == labels
    mask = jnp.any(hits, axis=2)
    share = jnp.sum(jnp.where(hits, probs[None], 0.0), axis=2)
    earlier = lax.broadcasted_iota(jnp.int32, (count, count), 1) < lax.broadcasted_iota(jnp.int32, (count, count), 0)
    place = jnp.sum(jnp.where(earlier[None] & mask[:, None, :], 1, 0), axis=2)
    slots = lax.broadcasted_iota(jnp.int32, (experts, SLOTS, count), 1)
    chosen = (place[:, None, :] == slots) & mask[:, None, :]
    pick = chosen.reshape(rows_of, count).astype(bf16)
    weight = jnp.where(first, jnp.ones_like(share), share)
    slot_weight = jnp.sum(jnp.where(chosen, weight[:, None, :], 0.0), axis=2).reshape(rows_of, 1)

    lines = count * narrow // LANES
    small = 2 * cells * CORES * count * narrow
    (sent,) = kernel(
        fan, [((cells * CORES, lines, LANES), bf16)], (0, small), None, tokens, grad_out, places=pltpu.HBM,
        scratch=[pltpu.VMEM((2, count, narrow), bf16), pltpu.SemaphoreType.DMA((2,))], room=ALL,
    )
    got = swap(sent, ("yh", "zh", "core"))

    big = 2 * units * width
    keep, send = kernel(
        arrange, [((near, 2 * units, wide), bf16)] * 2, (0, 8 * big), flag, w_gate[0], w_up[0], w_down[0]
    )
    (weights,) = kernel(join, [((near, 4 * units, wide), bf16)], (0, 8 * big), None, keep, across(send))

    block = ((near * experts, SLOTS, wide), bf16)
    (sent,) = kernel(dispatch, [block], (0, 2 * near * rows_of * wide), None, got, pick, slot_weight)
    got = swap(sent, ("yl", "zl", "expert"))
    mine = got.reshape(near, rows_of, wide)

    work = 2 * rows_of * 2 * big
    (proj,) = kernel(project, [((rows_of, 4 * units), f32)], (work, 6 * big), None, mine, weights)
    other = across(proj)
    (part,) = kernel(expand, [((near, rows_of, wide), bf16)], (work, 6 * big), flag, proj, other, weights)

    mine, part = lax.optimization_barrier((mine, part))
    grad_gate, grad_up, grad_down = kernel(
        weigh, [((units, width), bf16)] * 3, (work, 8 * big), flag, mine, across(mine), proj, other
    )
    got = swap(part.reshape(near * experts, SLOTS, wide), ("yl", "zl", "expert"))
    got, grad_gate, grad_up, grad_down = lax.optimization_barrier((got, grad_gate, grad_up, grad_down))
    back_weight = jnp.where(first, mask.astype(f32), share)
    spread = jnp.where(chosen, back_weight[:, None, :], 0.0).reshape(rows_of, count).T
    (sent,) = kernel(
        combine, [((cells * CORES, lines, LANES), bf16)], (0, 2 * near * rows_of * wide), None, got, spread
    )
    got = swap(sent, ("yh", "zh", "core"))
    grad_tokens, mixed = kernel(finish, [((count, narrow), bf16)] * 2, (0, small), None, got)

    return (mixed, grad_tokens, grad_gate[None], grad_up[None], grad_down[None])


def solution(mesh):
    dp, experts = mesh.devices.shape
    depth = dp // (COLUMNS * CORES)
    split = mesh.devices.reshape(COLUMNS // PAIR, PAIR, depth // PAIR, PAIR, CORES, experts)
    fine = Mesh(split, ("yh", "yl", "zh", "zl", "core", "expert"))
    dp = ("yh", "yl", "zh", "zl", "core")
    placed = (
        P("expert", dp),
        P("expert", None),
        P("expert", None),
        P("expert", dp, None),
        P("expert", dp, None),
        P("expert", dp, None),
        P("expert", dp),
    )
    return jax.shard_map(
        on_device,
        mesh=fine,
        in_specs=placed,
        out_specs=(P("expert", dp), P("expert", dp), P("expert", dp, None), P("expert", dp, None), P("expert", dp, None)),
        check_vma=False,
    )
```

time: 122 us -> 116 us (0.951)
  blocking collectives: 0 us -> 20.2 us
  waiting for transfers between devices: 55 us -> 40.3 us
  local copies, waits for them, and re-layouts: 12 us -> 2.25 us
  Pallas kernels: 4.93 us -> 11.7 us
  starting transfers between devices: 44.4 us -> 38.2 us
  other arithmetic: 3.35 us -> 1.76 us
    all_to_all x0 -> x1, blocking collectives: none -> 20.2 us  [swap(): return lax.all_to_all(a, axis, split_axis=0, concat_axis=0, tiled=True)]
    all_to_all x4 -> x3, waiting for transfers between devices: 51 us -> 33.7 us  [swap(): return lax.all_to_all(a, axis, split_axis=0, concat_axis=0, tiled=True)]
    pallas_call x4 -> x9, Pallas kernels: 4.93 us -> 11.7 us  [kernel(): pl.pallas_call(body, out_shape=tuple((jax.ShapeDtypeStruct(s, d) for s, d...]
    all_to_all x4 -> x3, starting transfers between devices: 36.2 us -> 30 us  [swap(): return lax.all_to_all(a, axis, split_axis=0, concat_axis=0, tiled=True)]
    unnamed x14 -> x8, local copies, waits for them, and re-layouts: 5.86 us -> 1.03 us
    ppermute x3, waiting for transfers between devices: 3.94 us -> 6.61 us  [across(): return lax.ppermute(a, 'core', [(0, 1), (1, 0)])]
    reshape x5 -> x1, local copies, waits for them, and re-layouts: 1.76 us -> 0.09 us  [on_device(): jnp.sum(jnp.where(chosen, weight[:, None, :], 0.0), axis=2)]
    broadcast_in_dim x2, local copies, waits for them, and re-layouts: 1.77 us -> 0.18 us  [on_device(): jnp.where(chosen, back_weight[:, None, :], 0.0).reshape(rows_of, count)]
  transfers between devices with their start and end apart: 7 -> 6, of which waited for: 6 -> 6; matrix products, arithmetic and copies ran while one was open for 4% -> 3% of each run, Pallas kernels for 2% -> 4%
where the time goes in v3:
time: 116 us; the launch traced here: 115 us
  waiting for transfers between devices  40.3 us (35%)
  starting transfers between devices  38.2 us (33%)
  blocking collectives  20.2 us (17%)
  Pallas kernels  11.7 us (10%)
  local copies, waits for them, and re-layouts  2.25 us (2%)
  other arithmetic  1.76 us (2%)
    all_to_all x3, waiting for transfers between devices, swap(): return lax.all_to_all(a, axis, split_axis=0, concat_axis=0, tiled=True)  33.7 us
    all_to_all x3, starting transfers between devices, swap(): return lax.all_to_all(a, axis, split_axis=0, concat_axis=0, tiled=True)  30 us
    all_to_all x1, blocking collectives, swap(): return lax.all_to_all(a, axis, split_axis=0, concat_axis=0, tiled=True)  20.2 us
    pallas_call x9, Pallas kernels, kernel(): pl.pallas_call(body, out_shape=tuple((jax.ShapeDtypeStruct(s, d) for s, d...  11.7 us
    ppermute x3, starting transfers between devices, across(): return lax.ppermute(a, 'core', [(0, 1), (1, 0)])  8.25 us
    ppermute x3, waiting for transfers between devices, across(): return lax.ppermute(a, 'core', [(0, 1), (1, 0)])  6.61 us
  transfers between devices with their start and end apart: 6, of which 6 were waited for; matrix products, arithmetic and copies ran while one was open for 3% of the time, Pallas kernels for 4%

profile of v3, /device:TPU:1, one launch (start us, length us, event | category | flops | bytes accessed | tf_op | source)
XLA Modules:
  0.0 115.3 jit_solution(5241970249963037506)
XLA Ops:
  0.6 1.5 %fan.1 = bf16[48,8,128]{2,1,0:T(8,128)(2,1)} custom-call(bf16[32,32]{1,0:T(8,128)(2,1)} %tokens_ref.1, bf16[32,32]{1,0:T(8,128)(2,1)} %grad_ref.1), custom_call_target="tpu_custom_call" | custom-call | bytes 98304 | tf_op jit(solution)/shard_map/fan/pallas_call | solution.py:218
  2.2 21.6 %all-to-all-start = ((bf16[48,8,128]{2,1,0:T(8,128)(2,1)}), bf16[48,8,128]{2,1,0:T(8,128)(2,1)S(1)}, u32[]{:S(2)}, u32[]{:S(2)}) async-start(bf16[48,8,128]{2,1,0:T(8,128)(2,1)} %fan.1), calls=%async_computation | async-start | bytes 196608 | tf_op jit(solution)/shard_map/all_to_all | solution.py:29
  23.8 0.7 fusion.1
  24.5 0.7 select_reduce_fusion.2
  25.2 0.1 copy.23
  25.3 0.1 select_reduce_fusion.1
  25.5 0.1 copy.22
  25.6 0.1 copy.24
  25.7 0.2 select_reduce_fusion
  25.9 0.1 iota.38
  25.9 0.1 and.31
  26.1 0.1 and.32
  26.2 0.1 copy.27
  26.2 0.1 reshape.55.weight_ref
  26.3 0.1 broadcast_in_dim.69
  26.4 0.1 broadcast_in_dim.70
  26.5 0.1 eq.27
  26.6 0.1 eq.28
  26.8 0.1 copy.25.pick_ref
  26.9 13.3 %all-to-all-done.got_ref = bf16[48,8,128]{2,1,0:T(8,128)(2,1)S(1)} async-done(((bf16[48,8,128]{2,1,0:T(8,128)(2,1)}), bf16[48,8,128]{2,1,0:T(8,128)(2,1)S(1)}, u32[]{:S(2)}, u32[]{:S(2)}) %all-to-all-start) | async-done | bytes 98336 | tf_op jit(solution)/shard_map/all_to_all | solution.py:29
  40.1 1.3 %dispatch.1 = bf16[16,24,1536]{2,1,0:T(8,128)(2,1)} custom-call(bf16[48,8,128]{2,1,0:T(8,128)(2,1)S(1)} %all-to-all-done.got_ref, bf16[96,32]{1,0:T(8,128)(2,1)S(1)} %copy.25.pick_ref, f32[96,1]{1,0:T(8,128)S(1)} %reshape.55.weight_ref), custom_call_target="tpu_custom_call" | custom-call | bytes 1179648 | tf_op jit(solution)/shard_map/dispatch/pallas_call | solution.py:218
  41.5 0.0 copy-start.1
  41.5 0.0 copy-start.2
  41.5 0.0 copy-start.3
  41.5 4.6 %all-to-all-start.1 = ((bf16[16,24,1536]{2,1,0:T(8,128)(2,1)}), bf16[16,24,1536]{2,1,0:T(8,128)(2,1)}, u32[]{:S(2)}, u32[]{:S(2)}) async-start(bf16[16,24,1536]{2,1,0:T(8,128)(2,1)} %dispatch.1), calls=%async_computation.1 | async-start | bytes 2359296 | tf_op jit(solution)/shard_map/all_to_all | solution.py:29
  46.1 0.0 copy-done.1
  46.1 0.0 copy-done.2
  46.1 0.0 copy-done.3
  46.2 0.7 arrange.1
  46.9 2.6 %collective-permute-start = (bf16[4,128,1536]{2,1,0:T(8,128)(2,1)S(1)}, bf16[4,128,1536]{2,1,0:T(8,128)(2,1)S(1)}, u32[]{:S(2)}, u32[]{:S(2)}) collective-permute-start(bf16[4,128,1536]{2,1,0:T(8,128)(2,1)S(1)} %get-tuple-element.19), channel_id=1, source_target_pairs={{0,4},{4,0},{1,5},{5,1},{2,6},{6,2},{3,7},{7,3},{8,12},{12,8},{9,1... | collective-permute-start | bytes 4718600 | tf_op jit(solution)/shard_map/ppermute | solution.py:33
  49.5 3.0 %collective-permute-done.recv_ref = bf16[4,128,1536]{2,1,0:T(8,128)(2,1)S(1)} collective-permute-done((bf16[4,128,1536]{2,1,0:T(8,128)(2,1)S(1)}, bf16[4,128,1536]{2,1,0:T(8,128)(2,1)S(1)}, u32[]{:S(2)}, u32[]{:S(2)}) %collective-permute-start) | collective-permute-done | bytes 1572896 | tf_op jit(solution)/shard_map/ppermute | solution.py:33
  52.5 0.2 join.1.weights_ref
  52.7 11.2 %all-to-all-done.1 = bf16[16,24,1536]{2,1,0:T(8,128)(2,1)} async-done(((bf16[16,24,1536]{2,1,0:T(8,128)(2,1)}), bf16[16,24,1536]{2,1,0:T(8,128)(2,1)}, u32[]{:S(2)}, u32[]{:S(2)}) %all-to-all-start.1) | async-done | bytes 1179680 | tf_op jit(solution)/shard_map/all_to_all | solution.py:29
  63.9 2.4 %project.1.mine_ref.here_ref = f32[96,256]{1,0:T(8,128)S(1)} custom-call(bf16[4,96,1536]{2,1,0:T(8,128)(2,1)} %bitcast.mine_ref, bf16[4,256,1536]{2,1,0:T(8,128)(2,1)S(1)} %join.1.weights_ref), custom_call_target="tpu_custom_call" | custom-call | flops 301989888 | bytes 4718592 | tf_op jit(solution)/shard_map/project/pallas_call | solution.py:218
  66.3 3.4 %collective-permute-start.1 = (f32[96,256]{1,0:T(8,128)S(1)}, f32[96,256]{1,0:T(8,128)S(1)}, u32[]{:S(2)}, u32[]{:S(2)}) collective-permute-start(f32[96,256]{1,0:T(8,128)S(1)} %project.1.mine_ref.here_ref), channel_id=1, source_target_pairs={{0,4},{4,0},{1,5},{5,1},{2,6},{6,2},{3,7},{7,3},{8,12},{12,8},{9,1... | collective-permute-start | bytes 294920 | tf_op jit(solution)/shard_map/ppermute | solution.py:33
  69.7 0.9 collective-permute-done.1.other_ref.there_ref
  70.6 0.7 expand.1
  71.3 0.0 copy-start
  71.3 1.0 copy-done
  72.4 3.7 %all-to-all-start.2 = ((bf16[16,24,1536]{2,1,0:T(8,128)(2,1)}), bf16[16,24,1536]{2,1,0:T(8,128)(2,1)S(1)}, u32[]{:S(2)}, u32[]{:S(2)}) async-start(bf16[16,24,1536]{2,1,0:T(8,128)(2,1)} %bitcast.17), calls=%async_computation.2 | async-start | bytes 2359296 | tf_op jit(solution)/shard_map/all_to_all | solution.py:29
  76.1 2.3 %collective-permute-start.2 = (bf16[4,96,1536]{2,1,0:T(8,128)(2,1)}, bf16[4,96,1536]{2,1,0:T(8,128)(2,1)S(1)}, u32[]{:S(2)}, u32[]{:S(2)}) collective-permute-start(bf16[4,96,1536]{2,1,0:T(8,128)(2,1)} %bitcast.mine_ref), channel_id=1, source_target_pairs={{0,4},{4,0},{1,5},{5,1},{2,6},{6,2},{3,7},{7,3},{8,12},{12,8},{9,1... | collective-permute-start | bytes 3538952 | tf_op jit(solution)/shard_map/ppermute | solution.py:33
  78.3 2.7 %collective-permute-done.2.other_ref = bf16[4,96,1536]{2,1,0:T(8,128)(2,1)S(1)} collective-permute-done((bf16[4,96,1536]{2,1,0:T(8,128)(2,1)}, bf16[4,96,1536]{2,1,0:T(8,128)(2,1)S(1)}, u32[]{:S(2)}, u32[]{:S(2)}) %collective-permute-start.2) | collective-permute-done | bytes 1179680 | tf_op jit(solution)/shard_map/ppermute | solution.py:33
  81.0 3.6 %weigh.1 = (bf16[64,6144]{1,0:T(8,128)(2,1)}, bf16[64,6144]{1,0:T(8,128)(2,1)}, bf16[64,6144]{1,0:T(8,128)(2,1)}) custom-call(s32[1]{0:T(128)} %bitcast.1.core_ref, bf16[4,96,1536]{2,1,0:T(8,128)(2,1)} %bitcast.mine_ref, bf16[4,96,1536]{2,1,0:T(8,128)(2,1)S(1)} %collective-permute-done.2.other_ref, f32[96,256]{1,0:T(8,128)S(1)} %project.1.mine_ref.here_ref, ...), custom_call_target="tpu_custom_call" | custom-call | flops 301989888 | bytes 6291456 | tf_op jit(solution)/shard_map/weigh/pallas_call | solution.py:218
  84.6 9.2 %all-to-all-done.2.got_ref = bf16[16,24,1536]{2,1,0:T(8,128)(2,1)S(1)} async-done(((bf16[16,24,1536]{2,1,0:T(8,128)(2,1)}), bf16[16,24,1536]{2,1,0:T(8,128)(2,1)S(1)}, u32[]{:S(2)}, u32[]{:S(2)}) %all-to-all-start.2) | async-done | bytes 1179680 | tf_op jit(solution)/shard_map/all_to_all | solution.py:29
  93.8 0.6 combine.1
  94.4 20.2 %all_to_all.20.got_ref = bf16[48,8,128]{2,1,0:T(8,128)(2,1)S(1)} all-to-all(bf16[48,8,128]{2,1,0:T(8,128)(2,1)S(1)} %combine.1), channel_id=1, replica_groups=mesh['yh'=4,'yl'=2,'zh'=6,'zl'=2,'core'=2,'expert'=4] {'yh','zh','core'}, dimensions={0} | all-to-all | bytes 196608 | tf_op jit(solution)/shard_map/all_to_all | solution.py:29
  114.6 0.7 finish.1
  (5 shorter events, 0.0 us)
Async XLA Ops:
  2.2 38.0 %all-to-all-start = ((bf16[48,8,128]{2,1,0:T(8,128)(2,1)}), bf16[48,8,128]{2,1,0:T(8,128)(2,1)S(1)}, u32[]{:S(2)}, u32[]{:S(2)}) async-start(bf16[48,8,128]{2,1,0:T(8,128)(2,1)} %fan.1), calls=%async_computation | async-start | bytes 196608 | tf_op jit(solution)/shard_map/all_to_all | solution.py:29
  41.5 4.7 %copy-start.1 = (bf16[1,64,6144]{2,1,0:T(8,128)(2,1)S(1)}, bf16[1,64,6144]{2,1,0:T(8,128)(2,1)}, u32[]{:S(2)}) copy-start(bf16[1,64,6144]{2,1,0:T(8,128)(2,1)} %param.10) | copy-start | bytes 2359300
  41.5 4.7 %copy-start.2 = (bf16[1,64,6144]{2,1,0:T(8,128)(2,1)S(1)}, bf16[1,64,6144]{2,1,0:T(8,128)(2,1)}, u32[]{:S(2)}) copy-start(bf16[1,64,6144]{2,1,0:T(8,128)(2,1)} %param.11) | copy-start | bytes 2359300
  41.5 4.7 %copy-start.3 = (bf16[1,64,6144]{2,1,0:T(8,128)(2,1)S(1)}, bf16[1,64,6144]{2,1,0:T(8,128)(2,1)}, u32[]{:S(2)}) copy-start(bf16[1,64,6144]{2,1,0:T(8,128)(2,1)} %param.12) | copy-start | bytes 2359300
  41.5 22.5 %all-to-all-start.1 = ((bf16[16,24,1536]{2,1,0:T(8,128)(2,1)}), bf16[16,24,1536]{2,1,0:T(8,128)(2,1)}, u32[]{:S(2)}, u32[]{:S(2)}) async-start(bf16[16,24,1536]{2,1,0:T(8,128)(2,1)} %dispatch.1), calls=%async_computation.1 | async-start | bytes 2359296 | tf_op jit(solution)/shard_map/all_to_all | solution.py:29
  46.9 5.6 %collective-permute-start = (bf16[4,128,1536]{2,1,0:T(8,128)(2,1)S(1)}, bf16[4,128,1536]{2,1,0:T(8,128)(2,1)S(1)}, u32[]{:S(2)}, u32[]{:S(2)}) collective-permute-start(bf16[4,128,1536]{2,1,0:T(8,128)(2,1)S(1)} %get-tuple-element.19), channel_id=1, source_target_pairs={{0,4},{4,0},{1,5},{5,1},{2,6},{6,2},{3,7},{7,3},{8,12},{12,8},{9,1... | collective-permute-start | bytes 4718600 | tf_op jit(solution)/shard_map/ppermute | solution.py:33
  66.3 4.3 %collective-permute-start.1 = (f32[96,256]{1,0:T(8,128)S(1)}, f32[96,256]{1,0:T(8,128)S(1)}, u32[]{:S(2)}, u32[]{:S(2)}) collective-permute-start(f32[96,256]{1,0:T(8,128)S(1)} %project.1.mine_ref.here_ref), channel_id=1, source_target_pairs={{0,4},{4,0},{1,5},{5,1},{2,6},{6,2},{3,7},{7,3},{8,12},{12,8},{9,1... | collective-permute-start | bytes 294920 | tf_op jit(solution)/shard_map/ppermute | solution.py:33
  71.3 1.0 copy-start
  72.4 21.5 %all-to-all-start.2 = ((bf16[16,24,1536]{2,1,0:T(8,128)(2,1)}), bf16[16,24,1536]{2,1,0:T(8,128)(2,1)S(1)}, u32[]{:S(2)}, u32[]{:S(2)}) async-start(bf16[16,24,1536]{2,1,0:T(8,128)(2,1)} %bitcast.17), calls=%async_computation.2 | async-start | bytes 2359296 | tf_op jit(solution)/shard_map/all_to_all | solution.py:29
  76.1 5.0 %collective-permute-start.2 = (bf16[4,96,1536]{2,1,0:T(8,128)(2,1)}, bf16[4,96,1536]{2,1,0:T(8,128)(2,1)S(1)}, u32[]{:S(2)}, u32[]{:S(2)}) collective-permute-start(bf16[4,96,1536]{2,1,0:T(8,128)(2,1)} %bitcast.mine_ref), channel_id=1, source_target_pairs={{0,4},{4,0},{1,5},{5,1},{2,6},{6,2},{3,7},{7,3},{8,12},{12,8},{9,1... | collective-permute-start | bytes 3538952 | tf_op jit(solution)/shard_map/ppermute | solution.py:33

commit v4 on v3

--- a/solution.py
+++ b/solution.py
@@ -69,20 +69,26 @@
         fill(send_ref, keep_ref)
 
 
-def join(keep_ref, recv_ref, out_ref):
-    n = keep_ref.shape[1]
-    for b in range(keep_ref.shape[0]):
-        out_ref[b, :n] = keep_ref[b]
-        out_ref[b, n:] = recv_ref[b]
-
-
-def project(mine_ref, weights_ref, out_ref):
-    n = weights_ref.shape[1] // 2
-    for at in (0, n):
-        total = ndot(mine_ref[0], weights_ref[0, at:at + n])
-        for b in range(1, mine_ref.shape[0]):
-            total = total + ndot(mine_ref[b], weights_ref[b, at:at + n])
-        out_ref[:, at:at + n] = total
+def settle(recv_ref, out_ref):
+    for b in range(recv_ref.shape[0]):
+        out_ref[b] = recv_ref[b]
+
+
+def product(mine_ref, weights_ref):
+    total = ndot(mine_ref[0], weights_ref[0])
+    for b in range(1, mine_ref.shape[0]):
+        total = total + ndot(mine_ref[b], weights_ref[b])
+    return total
+
+
+def project_own(mine_ref, keep_ref, out_ref):
+    out_ref[...] = product(mine_ref, keep_ref)
+
+
+def project_far(own_ref, mine_ref, far_ref, out_ref):
+    n = own_ref.shape[1]
+    out_ref[:, :n] = own_ref[...]
+    out_ref[:, n:] = product(mine_ref, far_ref)
 
 
 def activate(proj, dhid):
@@ -96,7 +102,7 @@
     return hidden, jnp.concatenate([dgate, dup], axis=1)
 
 
-def expand(core_ref, mine_ref, other_ref, weights_ref, part_ref):
+def expand(core_ref, mine_ref, other_ref, keep_ref, far_ref, part_ref):
     half = mine_ref.shape[1] // 2
     first = core_ref[0] == 0
     lefts = []
@@ -105,9 +111,9 @@
         hidden, pair = activate(jnp.where(first, here, there), jnp.where(first, there, here)[:, :half // 2])
         lone = jnp.concatenate([hidden, jnp.zeros_like(hidden)], axis=1)
         lefts.append(jnp.where(first, pair.astype(f32), lone.astype(f32)).astype(bf16))
-    left = jnp.concatenate(lefts, axis=1)
-    for b in range(weights_ref.shape[0]):
-        part_ref[b] = jnp.dot(left, weights_ref[b], preferred_element_type=f32).astype(bf16)
+    for b in range(keep_ref.shape[0]):
+        total = jnp.dot(lefts[0], keep_ref[b], preferred_element_type=f32)
+        part_ref[b] = (total + jnp.dot(lefts[1], far_ref[b], preferred_element_type=f32)).astype(bf16)
 
 
 def weigh(core_ref, mine_ref, other_ref, here_ref, there_ref, gate_ref, up_ref, down_ref):
@@ -263,7 +269,7 @@
     keep, send = kernel(
         arrange, [((near, 2 * units, wide), bf16)] * 2, (0, 8 * big), flag, w_gate[0], w_up[0], w_down[0]
     )
-    (weights,) = kernel(join, [((near, 4 * units, wide), bf16)], (0, 8 * big), None, keep, across(send))
+    (far,) = kernel(settle, [((near, 2 * units, wide), bf16)], (0, 4 * big), None, across(send))
 
     block = ((near * experts, SLOTS, wide), bf16)
     (sent,) = kernel(dispatch, [block], (0, 2 * near * rows_of * wide), None, got, pick, slot_weight)
@@ -271,9 +277,10 @@
     mine = got.reshape(near, rows_of, wide)
 
     work = 2 * rows_of * 2 * big
-    (proj,) = kernel(project, [((rows_of, 4 * units), f32)], (work, 6 * big), None, mine, weights)
+    (own,) = kernel(project_own, [((rows_of, 2 * units), f32)], (work // 2, 3 * big), None, mine, keep)
+    (proj,) = kernel(project_far, [((rows_of, 4 * units), f32)], (work // 2, 3 * big), None, own, mine, far)
     other = across(proj)
-    (part,) = kernel(expand, [((near, rows_of, wide), bf16)], (work, 6 * big), flag, proj, other, weights)
+    (part,) = kernel(expand, [((near, rows_of, wide), bf16)], (work, 6 * big), flag, proj, other, keep, far)
 
     mine, part = lax.optimization_barrier((mine, part))
     grad_gate, grad_up, grad_down = kernel(

time: 116 us -> 116 us (level)
  local copies, waits for them, and re-layouts: 2.25 us -> 4.8 us
  Pallas kernels: 11.7 us -> 9.35 us
    unnamed x8 -> x14, local copies, waits for them, and re-layouts: 1.03 us -> 3.58 us
    pallas_call x9 -> x10, Pallas kernels: 11.7 us -> 9.35 us  [kernel(): pl.pallas_call(body, out_shape=tuple((jax.ShapeDtypeStruct(s, d) for s, d...]
  transfers between devices with their start and end apart: 6 -> 6, of which waited for: 6 -> 6; matrix products, arithmetic and copies ran while one was open for 3% -> 3% of each run, Pallas kernels for 4% -> 3%
where the time goes in v4:
time: 116 us
  waiting for transfers between devices  40.5 us (35%)
  starting transfers between devices  38.2 us (33%)
  blocking collectives  20.2 us (17%)
  Pallas kernels  9.35 us (8%)
  local copies, waits for them, and re-layouts  4.8 us (4%)
  other arithmetic  1.76 us (2%)
    all_to_all x3, waiting for transfers between devices, swap(): return lax.all_to_all(a, axis, split_axis=0, concat_axis=0, tiled=True)  34.1 us
    all_to_all x3, starting transfers between devices, swap(): return lax.all_to_all(a, axis, split_axis=0, concat_axis=0, tiled=True)  29.9 us
    all_to_all x1, blocking collectives, swap(): return lax.all_to_all(a, axis, split_axis=0, concat_axis=0, tiled=True)  20.2 us
    pallas_call x10, Pallas kernels, kernel(): pl.pallas_call(body, out_shape=tuple((jax.ShapeDtypeStruct(s, d) for s, d...  9.35 us
    ppermute x3, starting transfers between devices, across(): return lax.ppermute(a, 'core', [(0, 1), (1, 0)])  8.25 us
    ppermute x3, waiting for transfers between devices, across(): return lax.ppermute(a, 'core', [(0, 1), (1, 0)])  6.4 us
    unnamed x14, local copies, waits for them, and re-layouts  3.58 us
  transfers between devices with their start and end apart: 6, of which 6 were waited for; matrix products, arithmetic and copies ran while one was open for 3% of the time, Pallas kernels for 3%

profile of v4, /device:TPU:1, one launch (start us, length us, event | category | flops | bytes accessed | tf_op | source)
XLA Modules:
  0.0 115.7 jit_solution(16828936216840543017)
XLA Ops:
  0.6 1.5 %fan.1 = bf16[48,8,128]{2,1,0:T(8,128)(2,1)} custom-call(bf16[32,32]{1,0:T(8,128)(2,1)} %tokens_ref.1, bf16[32,32]{1,0:T(8,128)(2,1)} %grad_ref.1), custom_call_target="tpu_custom_call" | custom-call | bytes 98304 | tf_op jit(solution)/shard_map/fan/pallas_call | solution.py:224
  2.2 21.6 %all-to-all-start = ((bf16[48,8,128]{2,1,0:T(8,128)(2,1)}), bf16[48,8,128]{2,1,0:T(8,128)(2,1)S(1)}, u32[]{:S(2)}, u32[]{:S(2)}) async-start(bf16[48,8,128]{2,1,0:T(8,128)(2,1)} %fan.1), calls=%async_computation | async-start | bytes 196608 | tf_op jit(solution)/shard_map/all_to_all | solution.py:29
  23.8 0.7 fusion.1
  24.5 0.7 select_reduce_fusion.2
  25.2 0.1 copy.23
  25.3 0.1 select_reduce_fusion.1
  25.5 0.1 copy.22
  25.6 0.1 copy.24
  25.7 0.2 select_reduce_fusion
  25.9 0.1 iota.38
  25.9 0.1 and.31
  26.1 0.1 and.32
  26.2 0.1 copy.27
  26.2 0.1 reshape.55.weight_ref
  26.3 0.1 broadcast_in_dim.69
  26.4 0.1 broadcast_in_dim.70
  26.5 0.1 eq.27
  26.6 0.1 eq.28
  26.8 0.1 copy.25.pick_ref
  26.9 13.3 %all-to-all-done.got_ref = bf16[48,8,128]{2,1,0:T(8,128)(2,1)S(1)} async-done(((bf16[48,8,128]{2,1,0:T(8,128)(2,1)}), bf16[48,8,128]{2,1,0:T(8,128)(2,1)S(1)}, u32[]{:S(2)}, u32[]{:S(2)}) %all-to-all-start) | async-done | bytes 98336 | tf_op jit(solution)/shard_map/all_to_all | solution.py:29
  40.1 1.3 %dispatch.1 = bf16[16,24,1536]{2,1,0:T(8,128)(2,1)} custom-call(bf16[48,8,128]{2,1,0:T(8,128)(2,1)S(1)} %all-to-all-done.got_ref, bf16[96,32]{1,0:T(8,128)(2,1)S(1)} %copy.25.pick_ref, f32[96,1]{1,0:T(8,128)S(1)} %reshape.55.weight_ref), custom_call_target="tpu_custom_call" | custom-call | bytes 1179648 | tf_op jit(solution)/shard_map/dispatch/pallas_call | solution.py:224
  41.5 0.0 copy-start.4
  41.5 0.0 copy-start.5
  41.5 0.0 copy-start.6
  41.5 4.6 %all-to-all-start.1 = ((bf16[16,24,1536]{2,1,0:T(8,128)(2,1)}), bf16[16,24,1536]{2,1,0:T(8,128)(2,1)S(1)}, u32[]{:S(2)}, u32[]{:S(2)}) async-start(bf16[16,24,1536]{2,1,0:T(8,128)(2,1)} %dispatch.1), calls=%async_computation.1 | async-start | bytes 2359296 | tf_op jit(solution)/shard_map/all_to_all | solution.py:29
  46.1 0.0 copy-done.4
  46.1 0.0 copy-done.5
  46.1 0.0 copy-done.6
  46.1 0.7 arrange.1
  46.8 0.0 copy-start
  46.9 1.1 copy-done
  48.0 2.6 %collective-permute-start = (bf16[4,128,1536]{2,1,0:T(8,128)(2,1)S(1)}, bf16[4,128,1536]{2,1,0:T(8,128)(2,1)S(1)}, u32[]{:S(2)}, u32[]{:S(2)}) collective-permute-start(bf16[4,128,1536]{2,1,0:T(8,128)(2,1)S(1)} %get-tuple-element.19), channel_id=1, source_target_pairs={{0,4},{4,0},{1,5},{5,1},{2,6},{6,2},{3,7},{7,3},{8,12},{12,8},{9,1... | collective-permute-start | bytes 4718600 | tf_op jit(solution)/shard_map/ppermute | solution.py:33
  50.6 3.0 %collective-permute-done.recv_ref = bf16[4,128,1536]{2,1,0:T(8,128)(2,1)S(1)} collective-permute-done((bf16[4,128,1536]{2,1,0:T(8,128)(2,1)S(1)}, bf16[4,128,1536]{2,1,0:T(8,128)(2,1)S(1)}, u32[]{:S(2)}, u32[]{:S(2)}) %collective-permute-start) | collective-permute-done | bytes 1572896 | tf_op jit(solution)/shard_map/ppermute | solution.py:33
  53.6 0.1 settle.1.far_ref
  53.7 10.1 %all-to-all-done.1 = bf16[16,24,1536]{2,1,0:T(8,128)(2,1)S(1)} async-done(((bf16[16,24,1536]{2,1,0:T(8,128)(2,1)}), bf16[16,24,1536]{2,1,0:T(8,128)(2,1)S(1)}, u32[]{:S(2)}, u32[]{:S(2)}) %all-to-all-start.1) | async-done | bytes 1179680 | tf_op jit(solution)/shard_map/all_to_all | solution.py:29
  63.9 0.0 copy-start.1
  63.9 1.4 %copy-done.1 = bf16[4,128,1536]{2,1,0:T(8,128)(2,1)S(1)} copy-done((bf16[4,128,1536]{2,1,0:T(8,128)(2,1)S(1)}, bf16[4,128,1536]{2,1,0:T(8,128)(2,1)}, u32[]{:S(2)}) %copy-start.1) | copy-done | bytes 1572888
  65.3 0.6 project_own.1.own_ref
  65.9 0.0 copy-start.2
  65.9 0.6 project_far.1.mine_ref.here_ref
  66.5 3.4 %collective-permute-start.1 = (f32[96,256]{1,0:T(8,128)S(1)}, f32[96,256]{1,0:T(8,128)S(1)}, u32[]{:S(2)}, u32[]{:S(2)}) collective-permute-start(f32[96,256]{1,0:T(8,128)S(1)} %project_far.1.mine_ref.here_ref), channel_id=1, source_target_pairs={{0,4},{4,0},{1,5},{5,1},{2,6},{6,2},{3,7},{7,3},{8,12},{12,8},{9,1... | collective-permute-start | bytes 294920 | tf_op jit(solution)/shard_map/ppermute | solution.py:33
  69.9 0.9 collective-permute-done.1.other_ref.there_ref
  70.8 0.0 copy-done.2
  70.8 0.8 expand.1
  71.7 0.0 copy-start.3
  71.7 1.0 copy-done.3
  72.7 3.7 %all-to-all-start.2 = ((bf16[16,24,1536]{2,1,0:T(8,128)(2,1)}), bf16[16,24,1536]{2,1,0:T(8,128)(2,1)S(1)}, u32[]{:S(2)}, u32[]{:S(2)}) async-start(bf16[16,24,1536]{2,1,0:T(8,128)(2,1)} %bitcast.21), calls=%async_computation.2 | async-start | bytes 2359296 | tf_op jit(solution)/shard_map/all_to_all | solution.py:29
  76.4 2.3 %collective-permute-start.2 = (bf16[4,96,1536]{2,1,0:T(8,128)(2,1)S(1)}, bf16[4,96,1536]{2,1,0:T(8,128)(2,1)S(1)}, u32[]{:S(2)}, u32[]{:S(2)}) collective-permute-start(bf16[4,96,1536]{2,1,0:T(8,128)(2,1)S(1)} %bitcast.19), channel_id=1, source_target_pairs={{0,4},{4,0},{1,5},{5,1},{2,6},{6,2},{3,7},{7,3},{8,12},{12,8},{9,1... | collective-permute-start | bytes 3538952 | tf_op jit(solution)/shard_map/ppermute | solution.py:33
  78.7 2.5 %collective-permute-done.2.other_ref = bf16[4,96,1536]{2,1,0:T(8,128)(2,1)S(1)} collective-permute-done((bf16[4,96,1536]{2,1,0:T(8,128)(2,1)S(1)}, bf16[4,96,1536]{2,1,0:T(8,128)(2,1)S(1)}, u32[]{:S(2)}, u32[]{:S(2)}) %collective-permute-start.2) | collective-permute-done | bytes 1179680 | tf_op jit(solution)/shard_map/ppermute | solution.py:33
  81.2 2.3 %weigh.1 = (bf16[64,6144]{1,0:T(8,128)(2,1)}, bf16[64,6144]{1,0:T(8,128)(2,1)}, bf16[64,6144]{1,0:T(8,128)(2,1)}) custom-call(s32[1]{0:T(128)} %bitcast.1.core_ref, bf16[4,96,1536]{2,1,0:T(8,128)(2,1)S(1)} %bitcast.20, bf16[4,96,1536]{2,1,0:T(8,128)(2,1)S(1)} %collective-permute-done.2.other_ref, f32[96,256]{1,0:T(8,128)S(1)} %project_far.1.mine_ref.here_ref, ...), custom_call_target="tpu_custom_call" | custom-call | flops 301989888 | bytes 6291456 | tf_op jit(solution)/shard_map/weigh/pallas_call | solution.py:224
  83.5 10.7 %all-to-all-done.2.got_ref = bf16[16,24,1536]{2,1,0:T(8,128)(2,1)S(1)} async-done(((bf16[16,24,1536]{2,1,0:T(8,128)(2,1)}), bf16[16,24,1536]{2,1,0:T(8,128)(2,1)S(1)}, u32[]{:S(2)}, u32[]{:S(2)}) %all-to-all-start.2) | async-done | bytes 1179680 | tf_op jit(solution)/shard_map/all_to_all | solution.py:29
  94.2 0.6 combine.1
  94.7 20.2 %all_to_all.20.got_ref = bf16[48,8,128]{2,1,0:T(8,128)(2,1)S(1)} all-to-all(bf16[48,8,128]{2,1,0:T(8,128)(2,1)S(1)} %combine.1), channel_id=1, replica_groups=mesh['yh'=4,'yl'=2,'zh'=6,'zl'=2,'core'=2,'expert'=4] {'yh','zh','core'}, dimensions={0} | all-to-all | bytes 196608 | tf_op jit(solution)/shard_map/all_to_all | solution.py:29
  115.0 0.7 finish.1
  (5 shorter events, 0.0 us)
Async XLA Ops:
  2.2 38.0 %all-to-all-start = ((bf16[48,8,128]{2,1,0:T(8,128)(2,1)}), bf16[48,8,128]{2,1,0:T(8,128)(2,1)S(1)}, u32[]{:S(2)}, u32[]{:S(2)}) async-start(bf16[48,8,128]{2,1,0:T(8,128)(2,1)} %fan.1), calls=%async_computation | async-start | bytes 196608 | tf_op jit(solution)/shard_map/all_to_all | solution.py:29
  41.5 4.6 %copy-start.4 = (bf16[1,64,6144]{2,1,0:T(8,128)(2,1)S(1)}, bf16[1,64,6144]{2,1,0:T(8,128)(2,1)}, u32[]{:S(2)}) copy-start(bf16[1,64,6144]{2,1,0:T(8,128)(2,1)} %param.10) | copy-start | bytes 2359300
  41.5 4.6 %copy-start.5 = (bf16[1,64,6144]{2,1,0:T(8,128)(2,1)S(1)}, bf16[1,64,6144]{2,1,0:T(8,128)(2,1)}, u32[]{:S(2)}) copy-start(bf16[1,64,6144]{2,1,0:T(8,128)(2,1)} %param.11) | copy-start | bytes 2359300
  41.5 4.6 %copy-start.6 = (bf16[1,64,6144]{2,1,0:T(8,128)(2,1)S(1)}, bf16[1,64,6144]{2,1,0:T(8,128)(2,1)}, u32[]{:S(2)}) copy-start(bf16[1,64,6144]{2,1,0:T(8,128)(2,1)} %param.12) | copy-start | bytes 2359300
  41.5 22.4 %all-to-all-start.1 = ((bf16[16,24,1536]{2,1,0:T(8,128)(2,1)}), bf16[16,24,1536]{2,1,0:T(8,128)(2,1)S(1)}, u32[]{:S(2)}, u32[]{:S(2)}) async-start(bf16[16,24,1536]{2,1,0:T(8,128)(2,1)} %dispatch.1), calls=%async_computation.1 | async-start | bytes 2359296 | tf_op jit(solution)/shard_map/all_to_all | solution.py:29
  46.8 1.1 copy-start
  48.0 5.6 %collective-permute-start = (bf16[4,128,1536]{2,1,0:T(8,128)(2,1)S(1)}, bf16[4,128,1536]{2,1,0:T(8,128)(2,1)S(1)}, u32[]{:S(2)}, u32[]{:S(2)}) collective-permute-start(bf16[4,128,1536]{2,1,0:T(8,128)(2,1)S(1)} %get-tuple-element.19), channel_id=1, source_target_pairs={{0,4},{4,0},{1,5},{5,1},{2,6},{6,2},{3,7},{7,3},{8,12},{12,8},{9,1... | collective-permute-start | bytes 4718600 | tf_op jit(solution)/shard_map/ppermute | solution.py:33
  63.9 1.4 %copy-start.1 = (bf16[4,128,1536]{2,1,0:T(8,128)(2,1)S(1)}, bf16[4,128,1536]{2,1,0:T(8,128)(2,1)}, u32[]{:S(2)}) copy-start(bf16[4,128,1536]{2,1,0:T(8,128)(2,1)} %copy-done) | copy-start | bytes 4718596
  65.9 5.0 %copy-start.2 = (bf16[4,128,1536]{2,1,0:T(8,128)(2,1)S(1)}, bf16[4,128,1536]{2,1,0:T(8,128)(2,1)}, u32[]{:S(2)}) copy-start(bf16[4,128,1536]{2,1,0:T(8,128)(2,1)} %copy-done) | copy-start | bytes 4718596
  66.5 4.3 %collective-permute-start.1 = (f32[96,256]{1,0:T(8,128)S(1)}, f32[96,256]{1,0:T(8,128)S(1)}, u32[]{:S(2)}, u32[]{:S(2)}) collective-permute-start(f32[96,256]{1,0:T(8,128)S(1)} %project_far.1.mine_ref.here_ref), channel_id=1, source_target_pairs={{0,4},{4,0},{1,5},{5,1},{2,6},{6,2},{3,7},{7,3},{8,12},{12,8},{9,1... | collective-permute-start | bytes 294920 | tf_op jit(solution)/shard_map/ppermute | solution.py:33
  71.7 1.0 copy-start.3
  72.7 21.5 %all-to-all-start.2 = ((bf16[16,24,1536]{2,1,0:T(8,128)(2,1)}), bf16[16,24,1536]{2,1,0:T(8,128)(2,1)S(1)}, u32[]{:S(2)}, u32[]{:S(2)}) async-start(bf16[16,24,1536]{2,1,0:T(8,128)(2,1)} %bitcast.21), calls=%async_computation.2 | async-start | bytes 2359296 | tf_op jit(solution)/shard_map/all_to_all | solution.py:29
  76.4 4.7 %collective-permute-start.2 = (bf16[4,96,1536]{2,1,0:T(8,128)(2,1)S(1)}, bf16[4,96,1536]{2,1,0:T(8,128)(2,1)S(1)}, u32[]{:S(2)}, u32[]{:S(2)}) collective-permute-start(bf16[4,96,1536]{2,1,0:T(8,128)(2,1)S(1)} %bitcast.19), channel_id=1, source_target_pairs={{0,4},{4,0},{1,5},{5,1},{2,6},{6,2},{3,7},{7,3},{8,12},{12,8},{9,1... | collective-permute-start | bytes 3538952 | tf_op jit(solution)/shard_map/ppermute | solution.py:33

commit v5 on v3

--- a/solution.py
+++ b/solution.py
@@ -76,7 +76,9 @@
         out_ref[b, n:] = recv_ref[b]
 
 
-def project(mine_ref, weights_ref, out_ref):
+def project(mine_ref, weights_ref, out_ref, rows_ref):
+    for b in range(mine_ref.shape[0]):
+        rows_ref[b] = mine_ref[b]
     n = weights_ref.shape[1] // 2
     for at in (0, n):
         total = ndot(mine_ref[0], weights_ref[0, at:at + n])
@@ -271,7 +273,8 @@
     mine = got.reshape(near, rows_of, wide)
 
     work = 2 * rows_of * 2 * big
-    (proj,) = kernel(project, [((rows_of, 4 * units), f32)], (work, 6 * big), None, mine, weights)
+    outs = [((rows_of, 4 * units), f32), ((near, rows_of, wide), bf16)]
+    proj, mine = kernel(project, outs, (work, 6 * big), None, mine, weights)
     other = across(proj)
     (part,) = kernel(expand, [((near, rows_of, wide), bf16)], (work, 6 * big), flag, proj, other, weights)
 

time: 116 us -> 117 us (level)
  waiting for transfers between devices: 40.3 us -> 41.6 us
  Pallas kernels: 11.7 us -> 10.5 us
    all_to_all x3, waiting for transfers between devices: 33.7 us -> 35.2 us  [swap(): return lax.all_to_all(a, axis, split_axis=0, concat_axis=0, tiled=True)]
    pallas_call x9, Pallas kernels: 11.7 us -> 10.5 us  [kernel(): pl.pallas_call(body, out_shape=tuple((jax.ShapeDtypeStruct(s, d) for s, d...]
  transfers between devices with their start and end apart: 6 -> 6, of which waited for: 6 -> 6; matrix products, arithmetic and copies ran while one was open for 3% -> 3% of each run, Pallas kernels for 4% -> 3%
where the time goes in v5:
time: 117 us
  waiting for transfers between devices  41.6 us (36%)
  starting transfers between devices  38.3 us (33%)
  blocking collectives  20.2 us (17%)
  Pallas kernels  10.5 us (9%)
  local copies, waits for them, and re-layouts  3.3 us (3%)
  other arithmetic  1.76 us (2%)
    all_to_all x3, waiting for transfers between devices, swap(): return lax.all_to_all(a, axis, split_axis=0, concat_axis=0, tiled=True)  35.2 us
    all_to_all x3, starting transfers between devices, swap(): return lax.all_to_all(a, axis, split_axis=0, concat_axis=0, tiled=True)  30.1 us
    all_to_all x1, blocking collectives, swap(): return lax.all_to_all(a, axis, split_axis=0, concat_axis=0, tiled=True)  20.2 us
    pallas_call x9, Pallas kernels, kernel(): pl.pallas_call(body, out_shape=tuple((jax.ShapeDtypeStruct(s, d) for s, d...  10.5 us
    ppermute x3, starting transfers between devices, across(): return lax.ppermute(a, 'core', [(0, 1), (1, 0)])  8.23 us
    ppermute x3, waiting for transfers between devices, across(): return lax.ppermute(a, 'core', [(0, 1), (1, 0)])  6.41 us
  transfers between devices with their start and end apart: 6, of which 6 were waited for; matrix products, arithmetic and copies ran while one was open for 3% of the time, Pallas kernels for 3%

profile of v5, /device:TPU:1, one launch (start us, length us, event | category | flops | bytes accessed | tf_op | source)
XLA Modules:
  0.0 116.6 jit_solution(3017753807435020896)
XLA Ops:
  0.6 1.5 %fan.1 = bf16[48,8,128]{2,1,0:T(8,128)(2,1)} custom-call(bf16[32,32]{1,0:T(8,128)(2,1)} %tokens_ref.1, bf16[32,32]{1,0:T(8,128)(2,1)} %grad_ref.1), custom_call_target="tpu_custom_call" | custom-call | bytes 98304 | tf_op jit(solution)/shard_map/fan/pallas_call | solution.py:220
  2.2 21.6 %all-to-all-start = ((bf16[48,8,128]{2,1,0:T(8,128)(2,1)}), bf16[48,8,128]{2,1,0:T(8,128)(2,1)S(1)}, u32[]{:S(2)}, u32[]{:S(2)}) async-start(bf16[48,8,128]{2,1,0:T(8,128)(2,1)} %fan.1), calls=%async_computation | async-start | bytes 196608 | tf_op jit(solution)/shard_map/all_to_all | solution.py:29
  23.8 0.7 fusion.1
  24.5 0.7 select_reduce_fusion.2
  25.2 0.1 copy.23
  25.3 0.1 select_reduce_fusion.1
  25.5 0.1 copy.22
  25.6 0.1 copy.24
  25.7 0.2 select_reduce_fusion
  25.9 0.1 iota.38
  25.9 0.1 and.31
  26.1 0.1 and.32
  26.2 0.1 copy.27
  26.2 0.1 reshape.55.weight_ref
  26.3 0.1 broadcast_in_dim.69
  26.4 0.1 broadcast_in_dim.70
  26.5 0.1 eq.27
  26.6 0.1 eq.28
  26.8 0.1 copy.25.pick_ref
  26.9 13.3 %all-to-all-done.got_ref = bf16[48,8,128]{2,1,0:T(8,128)(2,1)S(1)} async-done(((bf16[48,8,128]{2,1,0:T(8,128)(2,1)}), bf16[48,8,128]{2,1,0:T(8,128)(2,1)S(1)}, u32[]{:S(2)}, u32[]{:S(2)}) %all-to-all-start) | async-done | bytes 98336 | tf_op jit(solution)/shard_map/all_to_all | solution.py:29
  40.1 1.4 %dispatch.1 = bf16[16,24,1536]{2,1,0:T(8,128)(2,1)} custom-call(bf16[48,8,128]{2,1,0:T(8,128)(2,1)S(1)} %all-to-all-done.got_ref, bf16[96,32]{1,0:T(8,128)(2,1)S(1)} %copy.25.pick_ref, f32[96,1]{1,0:T(8,128)S(1)} %reshape.55.weight_ref), custom_call_target="tpu_custom_call" | custom-call | bytes 1179648 | tf_op jit(solution)/shard_map/dispatch/pallas_call | solution.py:220
  41.5 0.0 copy-start.3
  41.5 0.0 copy-start.4
  41.5 0.0 copy-start.5
  41.5 4.6 %all-to-all-start.1 = ((bf16[16,24,1536]{2,1,0:T(8,128)(2,1)}), bf16[16,24,1536]{2,1,0:T(8,128)(2,1)}, u32[]{:S(2)}, u32[]{:S(2)}) async-start(bf16[16,24,1536]{2,1,0:T(8,128)(2,1)} %dispatch.1), calls=%async_computation.1 | async-start | bytes 2359296 | tf_op jit(solution)/shard_map/all_to_all | solution.py:29
  46.1 0.0 copy-done.3
  46.2 0.0 copy-done.4
  46.2 0.0 copy-done.5
  46.2 0.7 arrange.1
  46.9 2.6 %collective-permute-start = (bf16[4,128,1536]{2,1,0:T(8,128)(2,1)S(1)}, bf16[4,128,1536]{2,1,0:T(8,128)(2,1)S(1)}, u32[]{:S(2)}, u32[]{:S(2)}) collective-permute-start(bf16[4,128,1536]{2,1,0:T(8,128)(2,1)S(1)} %get-tuple-element.21), channel_id=1, source_target_pairs={{0,4},{4,0},{1,5},{5,1},{2,6},{6,2},{3,7},{7,3},{8,12},{12,8},{9,1... | collective-permute-start | bytes 4718600 | tf_op jit(solution)/shard_map/ppermute | solution.py:33
  49.5 3.0 %collective-permute-done.recv_ref = bf16[4,128,1536]{2,1,0:T(8,128)(2,1)S(1)} collective-permute-done((bf16[4,128,1536]{2,1,0:T(8,128)(2,1)S(1)}, bf16[4,128,1536]{2,1,0:T(8,128)(2,1)S(1)}, u32[]{:S(2)}, u32[]{:S(2)}) %collective-permute-start) | collective-permute-done | bytes 1572896 | tf_op jit(solution)/shard_map/ppermute | solution.py:33
  52.5 0.2 join.1.weights_ref
  52.7 11.2 %all-to-all-done.1 = bf16[16,24,1536]{2,1,0:T(8,128)(2,1)} async-done(((bf16[16,24,1536]{2,1,0:T(8,128)(2,1)}), bf16[16,24,1536]{2,1,0:T(8,128)(2,1)}, u32[]{:S(2)}, u32[]{:S(2)}) %all-to-all-start.1) | async-done | bytes 1179680 | tf_op jit(solution)/shard_map/all_to_all | solution.py:29
  64.0 2.5 %project.1 = (f32[96,256]{1,0:T(8,128)S(1)}, bf16[4,96,1536]{2,1,0:T(8,128)(2,1)S(1)}) custom-call(bf16[4,96,1536]{2,1,0:T(8,128)(2,1)} %bitcast.mine_ref, bf16[4,256,1536]{2,1,0:T(8,128)(2,1)S(1)} %join.1.weights_ref), custom_call_target="tpu_custom_call" | custom-call | flops 301989888 | bytes 4718592 | tf_op jit(solution)/shard_map/project/pallas_call | solution.py:220
  66.4 0.0 copy-start.1
  66.4 1.0 copy-done.1
  67.5 3.4 %collective-permute-start.1 = (f32[96,256]{1,0:T(8,128)S(1)}, f32[96,256]{1,0:T(8,128)S(1)}, u32[]{:S(2)}, u32[]{:S(2)}) collective-permute-start(f32[96,256]{1,0:T(8,128)S(1)} %get-tuple-element.23.mine_ref.here_ref), channel_id=1, source_target_pairs={{0,4},{4,0},{1,5},{5,1},{2,6},{6,2},{3,7},{7,3},{8,12},{12,8},{9,1... | collective-permute-start | bytes 294920 | tf_op jit(solution)/shard_map/ppermute | solution.py:33
  70.8 0.9 collective-permute-done.1.other_ref.there_ref
  71.8 0.7 expand.1
  72.5 0.0 copy-start
  72.5 1.0 copy-done
  73.5 0.0 copy-start.2
  73.5 3.8 %all-to-all-start.2 = ((bf16[16,24,1536]{2,1,0:T(8,128)(2,1)}), bf16[16,24,1536]{2,1,0:T(8,128)(2,1)S(1)}, u32[]{:S(2)}, u32[]{:S(2)}) async-start(bf16[16,24,1536]{2,1,0:T(8,128)(2,1)} %bitcast.17), calls=%async_computation.2 | async-start | bytes 2359296 | tf_op jit(solution)/shard_map/all_to_all | solution.py:29
  77.3 0.0 copy-done.2
  77.3 2.3 %collective-permute-start.2 = (bf16[4,96,1536]{2,1,0:T(8,128)(2,1)S(1)}, bf16[4,96,1536]{2,1,0:T(8,128)(2,1)S(1)}, u32[]{:S(2)}, u32[]{:S(2)}) collective-permute-start(bf16[4,96,1536]{2,1,0:T(8,128)(2,1)S(1)} %copy-done.2), channel_id=1, source_target_pairs={{0,4},{4,0},{1,5},{5,1},{2,6},{6,2},{3,7},{7,3},{8,12},{12,8},{9,1... | collective-permute-start | bytes 3538952 | tf_op jit(solution)/shard_map/ppermute | solution.py:33
  79.6 2.5 %collective-permute-done.2.other_ref = bf16[4,96,1536]{2,1,0:T(8,128)(2,1)S(1)} collective-permute-done((bf16[4,96,1536]{2,1,0:T(8,128)(2,1)S(1)}, bf16[4,96,1536]{2,1,0:T(8,128)(2,1)S(1)}, u32[]{:S(2)}, u32[]{:S(2)}) %collective-permute-start.2) | collective-permute-done | bytes 1179680 | tf_op jit(solution)/shard_map/ppermute | solution.py:33
  82.1 2.3 %weigh.1 = (bf16[64,6144]{1,0:T(8,128)(2,1)}, bf16[64,6144]{1,0:T(8,128)(2,1)}, bf16[64,6144]{1,0:T(8,128)(2,1)}) custom-call(s32[1]{0:T(128)} %bitcast.1.core_ref, bf16[4,96,1536]{2,1,0:T(8,128)(2,1)S(1)} %copy-done.2, bf16[4,96,1536]{2,1,0:T(8,128)(2,1)S(1)} %collective-permute-done.2.other_ref, f32[96,256]{1,0:T(8,128)S(1)} %get-tuple-element.23.mine_ref.here_ref, ...), custom_call_target="tpu_custom_call" | custom-call | flops 301989888 | bytes 6291456 | tf_op jit(solution)/shard_map/weigh/pallas_call | solution.py:220
  84.4 10.7 %all-to-all-done.2.got_ref = bf16[16,24,1536]{2,1,0:T(8,128)(2,1)S(1)} async-done(((bf16[16,24,1536]{2,1,0:T(8,128)(2,1)}), bf16[16,24,1536]{2,1,0:T(8,128)(2,1)S(1)}, u32[]{:S(2)}, u32[]{:S(2)}) %all-to-all-start.2) | async-done | bytes 1179680 | tf_op jit(solution)/shard_map/all_to_all | solution.py:29
  95.1 0.6 combine.1
  95.7 20.2 %all_to_all.20.got_ref = bf16[48,8,128]{2,1,0:T(8,128)(2,1)S(1)} all-to-all(bf16[48,8,128]{2,1,0:T(8,128)(2,1)S(1)} %combine.1), channel_id=1, replica_groups=mesh['yh'=4,'yl'=2,'zh'=6,'zl'=2,'core'=2,'expert'=4] {'yh','zh','core'}, dimensions={0} | all-to-all | bytes 196608 | tf_op jit(solution)/shard_map/all_to_all | solution.py:29
  115.9 0.7 finish.1
  (5 shorter events, 0.0 us)
Async XLA Ops:
  2.2 38.0 %all-to-all-start = ((bf16[48,8,128]{2,1,0:T(8,128)(2,1)}), bf16[48,8,128]{2,1,0:T(8,128)(2,1)S(1)}, u32[]{:S(2)}, u32[]{:S(2)}) async-start(bf16[48,8,128]{2,1,0:T(8,128)(2,1)} %fan.1), calls=%async_computation | async-start | bytes 196608 | tf_op jit(solution)/shard_map/all_to_all | solution.py:29
  41.5 4.7 %copy-start.3 = (bf16[1,64,6144]{2,1,0:T(8,128)(2,1)S(1)}, bf16[1,64,6144]{2,1,0:T(8,128)(2,1)}, u32[]{:S(2)}) copy-start(bf16[1,64,6144]{2,1,0:T(8,128)(2,1)} %param.10) | copy-start | bytes 2359300
  41.5 4.7 %copy-start.4 = (bf16[1,64,6144]{2,1,0:T(8,128)(2,1)S(1)}, bf16[1,64,6144]{2,1,0:T(8,128)(2,1)}, u32[]{:S(2)}) copy-start(bf16[1,64,6144]{2,1,0:T(8,128)(2,1)} %param.11) | copy-start | bytes 2359300
  41.5 4.7 %copy-start.5 = (bf16[1,64,6144]{2,1,0:T(8,128)(2,1)S(1)}, bf16[1,64,6144]{2,1,0:T(8,128)(2,1)}, u32[]{:S(2)}) copy-start(bf16[1,64,6144]{2,1,0:T(8,128)(2,1)} %param.12) | copy-start | bytes 2359300
  41.5 22.5 %all-to-all-start.1 = ((bf16[16,24,1536]{2,1,0:T(8,128)(2,1)}), bf16[16,24,1536]{2,1,0:T(8,128)(2,1)}, u32[]{:S(2)}, u32[]{:S(2)}) async-start(bf16[16,24,1536]{2,1,0:T(8,128)(2,1)} %dispatch.1), calls=%async_computation.1 | async-start | bytes 2359296 | tf_op jit(solution)/shard_map/all_to_all | solution.py:29
  46.9 5.6 %collective-permute-start = (bf16[4,128,1536]{2,1,0:T(8,128)(2,1)S(1)}, bf16[4,128,1536]{2,1,0:T(8,128)(2,1)S(1)}, u32[]{:S(2)}, u32[]{:S(2)}) collective-permute-start(bf16[4,128,1536]{2,1,0:T(8,128)(2,1)S(1)} %get-tuple-element.21), channel_id=1, source_target_pairs={{0,4},{4,0},{1,5},{5,1},{2,6},{6,2},{3,7},{7,3},{8,12},{12,8},{9,1... | collective-permute-start | bytes 4718600 | tf_op jit(solution)/shard_map/ppermute | solution.py:33
  66.4 1.0 copy-start.1
  67.5 4.3 %collective-permute-start.1 = (f32[96,256]{1,0:T(8,128)S(1)}, f32[96,256]{1,0:T(8,128)S(1)}, u32[]{:S(2)}, u32[]{:S(2)}) collective-permute-start(f32[96,256]{1,0:T(8,128)S(1)} %get-tuple-element.23.mine_ref.here_ref), channel_id=1, source_target_pairs={{0,4},{4,0},{1,5},{5,1},{2,6},{6,2},{3,7},{7,3},{8,12},{12,8},{9,1... | collective-permute-start | bytes 294920 | tf_op jit(solution)/shard_map/ppermute | solution.py:33
  72.5 1.0 copy-start
  73.5 3.8 %copy-start.2 = (bf16[4,96,1536]{2,1,0:T(8,128)(2,1)S(1)}, bf16[4,96,1536]{2,1,0:T(8,128)(2,1)}, u32[]{:S(2)}) copy-start(bf16[4,96,1536]{2,1,0:T(8,128)(2,1)} %copy-done.1) | copy-start | bytes 3538948
  73.5 21.6 %all-to-all-start.2 = ((bf16[16,24,1536]{2,1,0:T(8,128)(2,1)}), bf16[16,24,1536]{2,1,0:T(8,128)(2,1)S(1)}, u32[]{:S(2)}, u32[]{:S(2)}) async-start(bf16[16,24,1536]{2,1,0:T(8,128)(2,1)} %bitcast.17), calls=%async_computation.2 | async-start | bytes 2359296 | tf_op jit(solution)/shard_map/all_to_all | solution.py:29
  77.3 4.7 %collective-permute-start.2 = (bf16[4,96,1536]{2,1,0:T(8,128)(2,1)S(1)}, bf16[4,96,1536]{2,1,0:T(8,128)(2,1)S(1)}, u32[]{:S(2)}, u32[]{:S(2)}) collective-permute-start(bf16[4,96,1536]{2,1,0:T(8,128)(2,1)S(1)} %copy-done.2), channel_id=1, source_target_pairs={{0,4},{4,0},{1,5},{5,1},{2,6},{6,2},{3,7},{7,3},{8,12},{12,8},{9,1... | collective-permute-start | bytes 3538952 | tf_op jit(solution)/shard_map/ppermute | solution.py:33
